TPU v7x, 128 devices: a whole 4x4x4 slice. The times are simulated.
128 devices in a mesh: gx: 32 (over x, y, z_hi), gy: 2 (over z_lo), gz: 2 (over core).
Axes of the slice: x: 4, y: 4, z: 4 (z_hi: 2, z_lo: 2; z = z_hi * 2 + z_lo), core: 2. Of those that a mesh axis runs over, the one named last changes fastest.
Arguments:
- initial: float32 [128, 256, 256], P('gx', 'gy', 'gz'), may hold values from -6 to 6
- material: int32 [128, 256, 256], P('gx', 'gy', 'gz'), may hold values from 0 to 7
- conduct: float32 [8], replicated, may hold values from 0.25 to 2
- capacity: float32 [8], replicated, may hold values from 1 to 4
- substeps: int32 [32, 2, 2], P('gx', 'gy', 'gz'), may hold values from 1 to 2
- trace_x: float32 [64, 2, 256, 256], P('gx', None, 'gy', 'gz'), may hold values from -12 to 12
- trace_y: float32 [2, 128, 4, 256], P(None, 'gx', 'gy', 'gz'), may hold values from -12 to 12
- trace_z: float32 [2, 4, 128, 256], P(None, 'gz', 'gx', 'gy'), may hold values from -12 to 12
Outputs:
- thermal_level_field: float32 [128, 256, 256], P('gx', 'gy', 'gz')
- converged_mixed_first: float32 [64, 2, 256, 256], P('gx', None, 'gy', 'gz')
- converged_mixed_second: float32 [2, 128, 4, 256], P(None, 'gx', 'gy', 'gz')
- converged_mixed_third: float32 [2, 4, 128, 256], P(None, 'gz', 'gx', 'gy')
Inputs may be any that keep to these rules, and one draw needn't show every extreme that they name: Each subdomain takes 1 or 2 substeps per coarse step.
All inputs are finite; a program needn't handle non-finite values.
Results may differ from a plain program's by a relative error of at most 0.0003.
Values sent between devices are 32-bit elements; how exact they have to be, the bound alone decides.
No kernel may reach another device: no remote copies, remote signals or barrier semaphores. Data moves between devices by JAX's collectives and lax.ppermute only.
A program may use at most 128 MiB of HBM per device.

v0:
```python
import functools

import jax
import jax.numpy as jnp
from jax import lax
from jax.experimental import pallas as pl
from jax.experimental.pallas import tpu as pltpu
from jax.sharding import PartitionSpec as P

NT = 2
SWEEPS = 8
ITERS = 4
NMAT = 8
SPAN_X = 4
SPAN = 128
SUB = 8
TURN = SPAN // SUB

p_robin = 1.5
dt_coarse = 0.5
rho_bound = 0.9

RHO2 = rho_bound**2
SHIFT = 1.0 - RHO2
QUAD = RHO2 * RHO2 / 4.0 + SHIFT
Y_ONE = 2.0 / RHO2 - 1.0
GAIN = 128.0 / (RHO2**4 * (8.0 * Y_ONE**4 - 8.0 * Y_ONE**2 + 1.0))

F32 = jnp.float32
FIELD = (TURN, SPAN_X, SUB, SPAN)
PLANE = (NT, TURN, SUB, SPAN)


def stride_rows(row):
    return pl.ds(row, SUB, stride=TURN)


def lanes():
    return lax.broadcasted_iota(jnp.int32, (SUB, SPAN), 1)


def sublanes():
    return lax.broadcasted_iota(jnp.int32, (SUB, SPAN), 0)


def harmonic(left_k, right_k):
    return 2.0 * left_k * right_k / (left_k + right_k)


def pick(bits, table_ref):
    level = [table_ref[i] for i in range(NMAT)]
    for bit in bits:
        level = [jnp.where(bit, level[2 * i + 1], level[2 * i]) for i in range(len(level) // 2)]
    return level[0]


def up_z(value):
    return pltpu.roll(value, SPAN - 1, 1)


def down_z(value):
    return pltpu.roll(value, 1, 1)


def up_y(value):
    return pltpu.roll(value, SUB - 1, 0)


def down_y(value):
    return pltpu.roll(value, 1, 0)


def prepare(steps, initial, material, conduct, capacity, cx, cy, cz, weight, scale, start, kcell):
    lane, sub = lanes(), sublanes()
    inverse_h = (steps.astype(F32)) * (1.0 / dt_coarse)
    for j in range(TURN):
        for x in range(SPAN_X):
            mat = material[x, stride_rows(j), :]
            bits = [(mat & 1) != 0, (mat & 2) != 0, (mat & 4) != 0]
            kcell[j, x] = pick(bits, conduct)
            start[j, x] = pick(bits, capacity)
    for j in range(TURN):
        for x in range(SPAN_X):
            here = kcell[j, x]
            if x < SPAN_X - 1:
                cx[j, x] = harmonic(here, kcell[j, x + 1])
            if j < TURN - 1:
                cy[j, x] = harmonic(here, kcell[j + 1, x])
            else:
                cy[j, x] = jnp.where(sub < SUB - 1, harmonic(here, up_y(kcell[0, x])), 0.0)
            cz[j, x] = jnp.where(lane < SPAN - 1, harmonic(here, up_z(here)), 0.0)
    for j in range(TURN):
        for x in range(SPAN_X):
            base = cz[j, x] + down_z(cz[j, x]) + cy[j, x]
            base = base + (cy[j - 1, x] if j > 0 else down_y(cy[TURN - 1, x]))
            if x < SPAN_X - 1:
                base = base + cx[j, x]
            if x > 0:
                base = base + cx[j, x - 1]
            if x in (0, SPAN_X - 1):
                base = base + p_robin
            base = base + jnp.where((lane == 0) | (lane == SPAN - 1), p_robin, 0.0)
            if j == 0:
                base = base + jnp.where(sub == 0, p_robin, 0.0)
            if j == TURN - 1:
                base = base + jnp.where(sub == SUB - 1, p_robin, 0.0)
            diagonal = start[j, x] * inverse_h + base
            root = lax.rsqrt(diagonal)
            root = root * (1.5 - 0.5 * diagonal * root * root)
            scale[j, x] = root
            weight[j, x] = -base * root * root
            start[j, x] = initial[x, stride_rows(j), :] * (diagonal * root)
    for j in range(TURN):
        for x in range(SPAN_X):
            here = scale[j, x]
            if x < SPAN_X - 1:
                cx[j, x] = cx[j, x] * here * scale[j, x + 1]
            after = scale[j + 1, x] if j < TURN - 1 else up_y(scale[0, x])
            cy[j, x] = cy[j, x] * here * after
            cz[j, x] = cz[j, x] * here * up_z(here)


def couple(cx, cy, cz, source, emit):
    last = [cy[TURN - 1, x] * source[TURN - 1, x] for x in range(SPAN_X)]
    before = [down_y(value) for value in last]
    here = [source[0, x] for x in range(SPAN_X)]
    first = here
    for j in range(TURN):
        if j < TURN - 1:
            after = [source[j + 1, x] for x in range(SPAN_X)]
        else:
            after = [up_y(value) for value in first]
        side = [cx[j, x] for x in range(SPAN_X - 1)]
        total, following = [], []
        for x in range(SPAN_X):
            link = cy[j, x]
            value = before[x] + link * after[x]
            following.append(link * here[x])
            link = cz[j, x]
            value = value + link * up_z(here[x])
            value = value + down_z(link * here[x])
            if x < SPAN_X - 1:
                value = value + side[x] * here[x + 1]
            if x > 0:
                value = value + side[x - 1] * here[x - 1]
            total.append(value)
        emit(j, here, total)
        before, here = following, after


def kernel(first, final, *refs):
    refs = list(refs)
    take = lambda n: [refs.pop(0) for _ in range(n)]
    (substeps,) = take(1)
    if first:
        initial, material, conduct, capacity, trace_x = take(5)
    else:
        cx, cy, cz, weight, scale, start, face_a, face_b, come_y, come_z = take(10)
    trace_y, trace_z = take(2)
    if first:
        cx, cy, cz, weight, scale, start = take(6)
    if final:
        (field_out,) = take(1)
    out_a, out_b, out_y, out_z = take(4)
    if first:
        kcell, face_a, face_b = take(3)
    field, load, res, one, two, three = take(6)
    rows_z, cols_z, sum_z, turn_z, sum_a, sum_b = take(6)

    steps = substeps[0]
    place_x, place_y, place_z = (lax.axis_index("gx"), lax.axis_index("gy"), lax.axis_index("gz"))
    odd = place_x % 2
    plane_a = (SPAN_X - 1) * (1 - odd)
    plane_b = (SPAN_X - 1) * odd
    edge = (place_x == 0) | (place_x == lax.axis_size("gx") - 1)
    part = jnp.where(steps == 2, F32(p_robin), F32(2.0 * p_robin))
    part_b = jnp.where(edge, F32(0.0), part)
    sign_b = jnp.where(edge, F32(1.0), F32(-1.0))
    lane, sub = lanes(), sublanes()

    if first:
        prepare(steps, initial, material, conduct, capacity, cx, cy, cz, weight, scale, start, kcell)
        for n in range(NT):
            for j in range(TURN):
                face_a[n, j] = trace_x[1 - odd, n, stride_rows(j), :]
                face_b[n, j] = trace_x[odd, n, stride_rows(j), :]

    rows_z[...] = jnp.zeros((SPAN, SPAN), F32)
    for n in range(NT):
        for x in range(SPAN_X):
            row = 2 * (SPAN_X * n + x)
            if first:
                rows_z[pl.ds(row, 1), :] = trace_z[n, 1, pl.ds(x, 1), :]
                rows_z[pl.ds(row + 1, 1), :] = trace_z[n, 0, pl.ds(x, 1), :]
            else:
                rows_z[pl.ds(row + place_z, 1), :] = come_z[n, pl.ds(x, 1), :]
                rows_z[pl.ds(row + 1 - place_z, 1), :] = trace_z[n, place_z, pl.ds(x, 1), :]
    cols_z[...] = rows_z[...].T
    for j in range(TURN):
        sum_z[j] = jnp.zeros((SUB, SPAN), F32)
        for x in range(SPAN_X):
            field[j, x] = start[j, x]

    def coarse(n, carry):
        for j in range(TURN):
            column = cols_z[stride_rows(j), :]
            for x in range(SPAN_X):
                turned = pltpu.roll(column, SPAN - 1 - 2 * x - 2 * SPAN_X * n, 1)
                value = jnp.where((lane == 0) | (lane == SPAN - 1), turned, 0.0)
                if j in (0, TURN - 1):
                    side = 0 if j == 0 else 1
                    kept = trace_y[n, x, pl.ds(side, 1), :]
                    if not first:
                        come = come_y[n, pl.ds(x, 1), :]
                        kept = jnp.where(place_y == side, kept, come)
                    at = 0 if j == 0 else SUB - 1
                    value = value + jnp.where(sub == at, kept, 0.0)
                load[j, x] = value * scale[j, x]
        for j in range(TURN):
            data = face_a[n, j]
            load[j, plane_a] = load[j, plane_a] + data * scale[j, plane_a]
            sum_a[j] = -data
            data = face_b[n, j]
            load[j, plane_b] = load[j, plane_b] + data * scale[j, plane_b]
            sum_b[j] = sign_b * data
        for x in range(SPAN_X):
            kept = trace_y[n, x, pl.ds(1 - place_y, 1), :] if first else come_y[n, pl.ds(x, 1), :]
            out_y[n, pl.ds(x, 1), :] = -kept

        def substep(_, carry):
            def to_res(j, here, total):
                for x in range(SPAN_X):
                    res[j, x] = total[x] + weight[j, x] * here[x] + load[j, x]

            def to_one(j, here, total):
                for x in range(SPAN_X):
                    one[j, x] = total[x] + here[x]

            def plain(target):
                def emit(j, here, total):
                    for x in range(SPAN_X):
                        target[j, x] = total[x]

                return emit

            def mixed(target, other, factor):
                def emit(j, here, total):
                    for x in range(SPAN_X):
                        target[j, x] = total[x] + factor * other[j, x]

                return emit

            def close(j, here, total):
                mask_z = lane // 2
                gathered = None
                for x in range(SPAN_X):
                    value = field[j, x] + GAIN * (total[x] + QUAD * res[j, x])
                    field[j, x] = value
                    value = value * scale[j, x]
                    turned = pltpu.roll(value, 1 + 2 * x + 2 * SPAN_X * n, 1)
                    chosen = jnp.where(mask_z == SPAN_X * n + x, turned, 0.0)
                    gathered = chosen if gathered is None else gathered + chosen
                    if j in (0, TURN - 1):
                        side = 0 if j == 0 else 1
                        at = 0 if j == 0 else SUB - 1

                        @pl.when(place_y != side)
                        def _():
                            line = out_y[n, pl.ds(x, 1), :]
                            out_y[n, pl.ds(x, 1), :] = line + part * value[at : at + 1, :]

                sum_z[j] = sum_z[j] + part * gathered
                sum_a[j] = sum_a[j] + part * (field[j, plane_a] * scale[j, plane_a])
                sum_b[j] = sum_b[j] + part_b * (field[j, plane_b] * scale[j, plane_b])

            couple(cx, cy, cz, field, to_res)
            couple(cx, cy, cz, res, to_one)
            couple(cx, cy, cz, one, plain(two))
            couple(cx, cy, cz, two, mixed(res, one, SHIFT))
            couple(cx, cy, cz, res, plain(one))
            couple(cx, cy, cz, one, mixed(two, res, -RHO2))
            couple(cx, cy, cz, two, plain(three))
            couple(cx, cy, cz, three, close)
            return carry

        lax.fori_loop(0, steps, substep, 0)
        for j in range(TURN):
            if final:
                out_a[n, stride_rows(j), :] = sum_a[j]
                out_b[n, stride_rows(j), :] = sum_b[j]
            else:
                out_a[n, j] = sum_a[j]
                out_b[n, j] = sum_b[j]
        return carry

    lax.fori_loop(0, NT, coarse, 0)

    for j in range(TURN):
        turn_z[stride_rows(j), :] = sum_z[j]
    cols_z[...] = turn_z[...].T
    for n in range(NT):
        for x in range(SPAN_X):
            row = 2 * (SPAN_X * n + x) + place_z
            out_z[n, pl.ds(x, 1), :] = cols_z[pl.ds(row, 1), :] - rows_z[pl.ds(row, 1), :]
    if final:
        for j in range(TURN):
            for x in range(SPAN_X):
                field_out[x, stride_rows(j), :] = field[j, x] * scale[j, x]


def solve(first, final, *operands):
    vmem = pl.BlockSpec(memory_space=pltpu.VMEM)
    smem = pl.BlockSpec(memory_space=pltpu.SMEM)
    if first:
        in_specs = [smem, vmem, vmem, smem, smem] + [vmem] * 3
    else:
        in_specs = [smem] + [vmem] * 12
    shapes = []
    if first:
        shapes += [(TURN, SPAN_X - 1, SUB, SPAN)] + [FIELD] * 5
    if final:
        shapes += [(SPAN_X, SPAN, SPAN)]
    shapes += [(NT, SPAN, SPAN) if final else PLANE] * 2
    shapes += [(NT, SPAN_X, SPAN)] * 2
    scratch = ([FIELD, PLANE, PLANE] if first else []) + [FIELD] * 6
    scratch += [(SPAN, SPAN), (SPAN, SPAN), (TURN, SUB, SPAN), (SPAN, SPAN), (TURN, SUB, SPAN), (TURN, SUB, SPAN)]
    return pl.pallas_call(
        functools.partial(kernel, first, final),
        out_shape=[jax.ShapeDtypeStruct(shape, F32) for shape in shapes],
        in_specs=in_specs,
        out_specs=[vmem] * len(shapes),
        scratch_shapes=[pltpu.VMEM(shape, F32) for shape in scratch],
        compiler_params=pltpu.CompilerParams(vmem_limit_bytes=24 * 1024 * 1024),
    )(*operands)


def exchange(out_a, out_b, out_y, out_z):
    count = lax.axis_size("gx")
    pairs_a = [(i, i ^ 1) for i in range(count)]
    pairs_b = [(0, 0)] + [(i, i + 1 if i % 2 else i - 1) for i in range(1, count - 1)] + [(count - 1, count - 1)]
    swap = [(0, 1), (1, 0)]
    return (
        lax.ppermute(out_a, "gx", pairs_a),
        lax.ppermute(out_b, "gx", pairs_b),
        lax.ppermute(out_y, "gy", swap),
        lax.ppermute(out_z, "gz", swap),
    )


def local(initial, material, conduct, capacity, substeps, trace_x, trace_y, trace_z):
    steps = substeps.reshape(1)
    odd = lax.axis_index("gx") % 2
    place_y, place_z = (lax.axis_index("gy"), lax.axis_index("gz"))
    results = solve(True, False, steps, initial, material, conduct, capacity, trace_x, trace_y, trace_z)
    prepared, sent = results[:6], results[6:]
    for iteration in range(1, ITERS):
        arrived = exchange(*sent)
        final = iteration == ITERS - 1
        sent = solve(False, final, steps, *prepared, *arrived, trace_y, trace_z)
    field, *sent = sent
    face_a, face_b, come_y, come_z = exchange(*sent)
    got_x = jnp.stack([jnp.where(odd == 1, face_a, face_b), jnp.where(odd == 1, face_b, face_a)], 0)
    got_y = jnp.stack([jnp.where(place_y == side, trace_y[:, :, side], come_y) for side in range(2)], 2)
    got_z = jnp.stack([jnp.where(place_z == side, trace_z[:, side], come_z) for side in range(2)], 1)
    return (field, got_x, got_y, got_z)


def solution(mesh):
    placed = (
        P("gx", "gy", "gz"),
        P("gx", "gy", "gz"),
        P(),
        P(),
        P("gx", "gy", "gz"),
        P("gx", None, "gy", "gz"),
        P(None, "gx", "gy", "gz"),
        P(None, "gz", "gx", "gy"),
    )
    return jax.shard_map(
        local,
        mesh=mesh,
        in_specs=placed,
        out_specs=(
            P("gx", "gy", "gz"),
            P("gx", None, "gy", "gz"),
            P(None, "gx", "gy", "gz"),
            P(None, "gz", "gx", "gy"),
        ),
        check_vma=False,
    )
```

profile of v0, /device:TPU:3, one launch (start us, length us, event | category | flops | bytes accessed | tf_op | source)
XLA Modules:
  0.0 96.2 jit_solution(12936855792155478377)
XLA Ops:
  1.3 0.0 copy-start.6
  1.3 0.0 copy-start.7
  1.3 0.6 copy-done.6
  1.9 0.0 copy-done.7
  2.0 0.0 copy-start
  2.0 0.9 copy-done
  2.9 0.0 copy-start.1
  2.9 0.9 copy-done.1
  3.9 0.0 copy-start.2
  3.9 0.9 copy-done.2
  4.8 0.0 copy-start.3
  4.8 0.7 copy-done.3
  5.5 0.0 copy-start.4
  5.5 0.7 copy-done.4
  6.2 10.0 %shard_map.111 = (f32[16,3,8,128]{3,2,1,0:T(8,128)S(1)}, f32[16,4,8,128]{3,2,1,0:T(8,128)S(1)}, f32[16,4,8,128]{3,2,1,0:T(8,128)S(1)}, f32[16,4,8,128]{3,2,1,0:T...) custom-call(s32[1]{0:T(128)} %bitcast.31.refs_0_, ...), custom_call_target="tpu_custom_call" | custom-call | tf_op jit(solution)/shard_map/pallas_call | solution.py:327
  16.2 3.7 %collective-permute-start = (f32[2,16,8,128]{3,2,1,0:T(8,128)S(1)}, f32[2,16,8,128]{3,2,1,0:T(8,128)S(1)}, u32[]{:S(2)}, u32[]{:S(2)}) collective-permute-start(f32[2,16,8,128]{3,2,1,0:T(8,128)S(1)} %get-tuple-element.33), channel_id=1, source_target_pairs={{0,4},{4,0},{8,12},{12,8},{16,20},{20,16},{24,28},{28,24},{32,36},... | collective-permute-start | bytes 393224 | tf_op jit(solution)/shard_map/ppermute | solution.py:343
  19.9 4.3 %collective-permute-start.1 = (f32[2,16,8,128]{3,2,1,0:T(8,128)S(1)}, f32[2,16,8,128]{3,2,1,0:T(8,128)S(1)}, u32[]{:S(2)}, u32[]{:S(2)}) collective-permute-start(f32[2,16,8,128]{3,2,1,0:T(8,128)S(1)} %get-tuple-element.34), channel_id=1, source_target_pairs={{0,0},{4,8},{8,4},{12,16},{16,12},{20,24},{24,20},{28,32},{32,28},... | collective-permute-start | bytes 393224 | tf_op jit(solution)/shard_map/ppermute | solution.py:344
  24.2 1.1 %collective-permute-start.2 = (f32[2,4,128]{2,1,0:T(4,128)S(1)}, f32[2,4,128]{2,1,0:T(4,128)S(1)}, u32[]{:S(2)}, u32[]{:S(2)}) collective-permute-start(f32[2,4,128]{2,1,0:T(4,128)S(1)} %get-tuple-element.35), channel_id=1, source_target_pairs={{0,2},{2,0},{1,3},{3,1},{4,6},{6,4},{5,7},{7,5},{8,10},{10,8},{9,1... | collective-permute-start | bytes 12296 | tf_op jit(solution)/shard_map/ppermute | solution.py:345
  25.3 1.5 %collective-permute-start.3 = (f32[2,4,128]{2,1,0:T(4,128)S(1)}, f32[2,4,128]{2,1,0:T(4,128)S(1)}, u32[]{:S(2)}, u32[]{:S(2)}) collective-permute-start(f32[2,4,128]{2,1,0:T(4,128)S(1)} %get-tuple-element.36), channel_id=1, source_target_pairs={{0,1},{1,0},{2,3},{3,2},{4,5},{5,4},{6,7},{7,6},{8,9},{9,8},{10,11... | collective-permute-start | bytes 12296 | tf_op jit(solution)/shard_map/ppermute | solution.py:346
  26.8 0.4 collective-permute-done.2.refs_9_
  27.2 0.5 collective-permute-done.3.refs_10_
  27.6 0.0 collective-permute-done.refs_7_
  27.6 2.5 %collective-permute-done.1.refs_8_ = f32[2,16,8,128]{3,2,1,0:T(8,128)S(1)} collective-permute-done((f32[2,16,8,128]{3,2,1,0:T(8,128)S(1)}, f32[2,16,8,128]{3,2,1,0:T(8,128)S(1)}, u32[]{:S(2)}, u32[]{:S(2)}) %collective-permute-start.1) | collective-permute-done | bytes 131104 | tf_op jit(solution)/shard_map/ppermute | solution.py:344
  30.1 8.8 %shard_map.112 = (f32[2,16,8,128]{3,2,1,0:T(8,128)S(1)}, f32[2,16,8,128]{3,2,1,0:T(8,128)S(1)}, f32[2,4,128]{2,1,0:T(4,128)S(1)}, f32[2,4,128]{2,1,0:T(4,128)S(1)}) custom-call(s32[1]{0:T(128)} %bitcast.32.refs_0_, f32[16,3,8,128]{3,2,1,0:T(8,128)S(1)} %get-tuple-element.27.refs_1_, f32[16,4,8,128]{3,2,1,0:T(8,128)S(1)} %get-tuple-element.28.refs_2_, ...), custom_call_target="tpu_custom_call" | custom-call | tf_op jit(solution)/shard_map/pallas_call | solution.py:327
  38.9 0.1 collective-permute-start.4
  39.0 5.2 %collective-permute-start.5 = (f32[2,16,8,128]{3,2,1,0:T(8,128)S(1)}, f32[2,16,8,128]{3,2,1,0:T(8,128)S(1)}, u32[]{:S(2)}, u32[]{:S(2)}) collective-permute-start(f32[2,16,8,128]{3,2,1,0:T(8,128)S(1)} %get-tuple-element.38), channel_id=1, source_target_pairs={{0,0},{4,8},{8,4},{12,16},{16,12},{20,24},{24,20},{28,32},{32,28},... | collective-permute-start | bytes 393224 | tf_op jit(solution)/shard_map/ppermute | solution.py:344
  44.2 0.1 collective-permute-start.6
  44.3 3.7 %collective-permute-start.7 = (f32[2,4,128]{2,1,0:T(4,128)S(1)}, f32[2,4,128]{2,1,0:T(4,128)S(1)}, u32[]{:S(2)}, u32[]{:S(2)}) collective-permute-start(f32[2,4,128]{2,1,0:T(4,128)S(1)} %get-tuple-element.40), channel_id=1, source_target_pairs={{0,1},{1,0},{2,3},{3,2},{4,5},{5,4},{6,7},{7,6},{8,9},{9,8},{10,11... | collective-permute-start | bytes 12296 | tf_op jit(solution)/shard_map/ppermute | solution.py:346
  47.9 0.0 collective-permute-done.6.refs_9_
  47.9 0.8 collective-permute-done.7.refs_10_
  48.8 0.0 collective-permute-done.4.refs_7_
  48.8 0.5 collective-permute-done.5.refs_8_
  49.2 8.8 %shard_map.113 = (f32[2,16,8,128]{3,2,1,0:T(8,128)S(1)}, f32[2,16,8,128]{3,2,1,0:T(8,128)S(1)}, f32[2,4,128]{2,1,0:T(4,128)S(1)}, f32[2,4,128]{2,1,0:T(4,128)S(1)}) custom-call(s32[1]{0:T(128)} %bitcast.33.refs_0_, f32[16,3,8,128]{3,2,1,0:T(8,128)S(1)} %get-tuple-element.27.refs_1_, f32[16,4,8,128]{3,2,1,0:T(8,128)S(1)} %get-tuple-element.28.refs_2_, ...), custom_call_target="tpu_custom_call" | custom-call | tf_op jit(solution)/shard_map/pallas_call | solution.py:327
  58.0 0.9 collective-permute-start.8
  58.9 4.8 %collective-permute-start.9 = (f32[2,16,8,128]{3,2,1,0:T(8,128)S(1)}, f32[2,16,8,128]{3,2,1,0:T(8,128)S(1)}, u32[]{:S(2)}, u32[]{:S(2)}) collective-permute-start(f32[2,16,8,128]{3,2,1,0:T(8,128)S(1)} %get-tuple-element.42), channel_id=1, source_target_pairs={{0,0},{4,8},{8,4},{12,16},{16,12},{20,24},{24,20},{28,32},{32,28},... | collective-permute-start | bytes 393224 | tf_op jit(solution)/shard_map/ppermute | solution.py:344
  63.8 0.1 collective-permute-start.10
  63.9 4.8 %collective-permute-start.11 = (f32[2,4,128]{2,1,0:T(4,128)S(1)}, f32[2,4,128]{2,1,0:T(4,128)S(1)}, u32[]{:S(2)}, u32[]{:S(2)}) collective-permute-start(f32[2,4,128]{2,1,0:T(4,128)S(1)} %get-tuple-element.44), channel_id=1, source_target_pairs={{0,1},{1,0},{2,3},{3,2},{4,5},{5,4},{6,7},{7,6},{8,9},{9,8},{10,11... | collective-permute-start | bytes 12296 | tf_op jit(solution)/shard_map/ppermute | solution.py:346
  68.7 0.0 collective-permute-done.10.refs_9_
  68.7 0.8 collective-permute-done.11.refs_10_
  69.5 0.0 collective-permute-done.8.refs_7_
  69.5 0.0 collective-permute-done.9.refs_8_
  69.5 9.6 %shard_map.114 = (f32[4,128,128]{2,1,0:T(8,128)}, f32[2,128,128]{2,1,0:T(8,128)S(1)}, f32[2,128,128]{2,1,0:T(8,128)S(1)}, f32[2,4,128]{2,1,0:T(4,128)S(1)}, f32[2,4,128]{2,1,0:T(4,128)S(1)}) custom-call(s32[1]{0:T(128)} %bitcast.34.refs_0_, f32[16,3,8,128]{3,2,1,0:T(8,128)S(1)} %get-tuple-element.27.refs_1_, ...), custom_call_target="tpu_custom_call" | custom-call | tf_op jit(solution)/shard_map/pallas_call | solution.py:327
  79.1 4.6 %collective-permute-start.15 = (f32[2,4,128]{2,1,0:T(4,128)S(1)}, f32[2,4,128]{2,1,0:T(4,128)S(1)}, u32[]{:S(2)}, u32[]{:S(2)}) collective-permute-start(f32[2,4,128]{2,1,0:T(4,128)S(1)} %get-tuple-element.49), channel_id=1, source_target_pairs={{0,1},{1,0},{2,3},{3,2},{4,5},{5,4},{6,7},{7,6},{8,9},{9,8},{10,11... | collective-permute-start | bytes 12296 | tf_op jit(solution)/shard_map/ppermute | solution.py:346
  83.7 0.0 copy-start.5
  83.7 0.1 collective-permute-start.14
  83.8 0.1 collective-permute-start.12
  83.9 5.8 %collective-permute-start.13 = (f32[2,128,128]{2,1,0:T(8,128)S(1)}, f32[2,128,128]{2,1,0:T(8,128)S(1)}, u32[]{:S(2)}, u32[]{:S(2)}) collective-permute-start(f32[2,128,128]{2,1,0:T(8,128)S(1)} %get-tuple-element.47), channel_id=1, source_target_pairs={{0,0},{4,8},{8,4},{12,16},{16,12},{20,24},{24,20},{28,32},{32,28},... | collective-permute-start | bytes 393224 | tf_op jit(solution)/shard_map/ppermute | solution.py:344
  89.8 0.0 collective-permute-done.15
  89.8 0.0 copy-done.5
  89.8 0.0 collective-permute-done.14
  89.8 0.6 copy.17
  90.4 0.6 copy.16
  91.0 0.0 collective-permute-done.12
  91.0 4.4 %collective-permute-done.13 = f32[2,128,128]{2,1,0:T(8,128)S(1)} collective-permute-done((f32[2,128,128]{2,1,0:T(8,128)S(1)}, f32[2,128,128]{2,1,0:T(8,128)S(1)}, u32[]{:S(2)}, u32[]{:S(2)}) %collective-permute-start.13) | collective-permute-done | bytes 131104 | tf_op jit(solution)/shard_map/ppermute | solution.py:344
  95.5 0.7 pad_maximum_fusion
  (6 shorter events, 0.1 us)
Async XLA Ops:
  1.3 0.7 copy-start.6
  1.3 0.7 copy-start.7
  2.0 0.9 copy-start
  2.9 0.9 copy-start.1
  3.9 0.9 copy-start.2
  4.8 0.7 copy-start.3
  5.5 0.7 copy-start.4
  16.2 11.4 %collective-permute-start = (f32[2,16,8,128]{3,2,1,0:T(8,128)S(1)}, f32[2,16,8,128]{3,2,1,0:T(8,128)S(1)}, u32[]{:S(2)}, u32[]{:S(2)}) collective-permute-start(f32[2,16,8,128]{3,2,1,0:T(8,128)S(1)} %get-tuple-element.33), channel_id=1, source_target_pairs={{0,4},{4,0},{8,12},{12,8},{16,20},{20,16},{24,28},{28,24},{32,36},... | collective-permute-start | bytes 393224 | tf_op jit(solution)/shard_map/ppermute | solution.py:343
  19.9 10.2 %collective-permute-start.1 = (f32[2,16,8,128]{3,2,1,0:T(8,128)S(1)}, f32[2,16,8,128]{3,2,1,0:T(8,128)S(1)}, u32[]{:S(2)}, u32[]{:S(2)}) collective-permute-start(f32[2,16,8,128]{3,2,1,0:T(8,128)S(1)} %get-tuple-element.34), channel_id=1, source_target_pairs={{0,0},{4,8},{8,4},{12,16},{16,12},{20,24},{24,20},{28,32},{32,28},... | collective-permute-start | bytes 393224 | tf_op jit(solution)/shard_map/ppermute | solution.py:344
  24.2 2.9 %collective-permute-start.2 = (f32[2,4,128]{2,1,0:T(4,128)S(1)}, f32[2,4,128]{2,1,0:T(4,128)S(1)}, u32[]{:S(2)}, u32[]{:S(2)}) collective-permute-start(f32[2,4,128]{2,1,0:T(4,128)S(1)} %get-tuple-element.35), channel_id=1, source_target_pairs={{0,2},{2,0},{1,3},{3,1},{4,6},{6,4},{5,7},{7,5},{8,10},{10,8},{9,1... | collective-permute-start | bytes 12296 | tf_op jit(solution)/shard_map/ppermute | solution.py:345
  25.3 2.3 %collective-permute-start.3 = (f32[2,4,128]{2,1,0:T(4,128)S(1)}, f32[2,4,128]{2,1,0:T(4,128)S(1)}, u32[]{:S(2)}, u32[]{:S(2)}) collective-permute-start(f32[2,4,128]{2,1,0:T(4,128)S(1)} %get-tuple-element.36), channel_id=1, source_target_pairs={{0,1},{1,0},{2,3},{3,2},{4,5},{5,4},{6,7},{7,6},{8,9},{9,8},{10,11... | collective-permute-start | bytes 12296 | tf_op jit(solution)/shard_map/ppermute | solution.py:346
  38.9 9.9 %collective-permute-start.4 = (f32[2,16,8,128]{3,2,1,0:T(8,128)S(1)}, f32[2,16,8,128]{3,2,1,0:T(8,128)S(1)}, u32[]{:S(2)}, u32[]{:S(2)}) collective-permute-start(f32[2,16,8,128]{3,2,1,0:T(8,128)S(1)} %get-tuple-element.37), channel_id=1, source_target_pairs={{0,4},{4,0},{8,12},{12,8},{16,20},{20,16},{24,28},{28,24},{32,36},... | collective-permute-start | bytes 393224 | tf_op jit(solution)/shard_map/ppermute | solution.py:343
  39.0 10.3 %collective-permute-start.5 = (f32[2,16,8,128]{3,2,1,0:T(8,128)S(1)}, f32[2,16,8,128]{3,2,1,0:T(8,128)S(1)}, u32[]{:S(2)}, u32[]{:S(2)}) collective-permute-start(f32[2,16,8,128]{3,2,1,0:T(8,128)S(1)} %get-tuple-element.38), channel_id=1, source_target_pairs={{0,0},{4,8},{8,4},{12,16},{16,12},{20,24},{24,20},{28,32},{32,28},... | collective-permute-start | bytes 393224 | tf_op jit(solution)/shard_map/ppermute | solution.py:344
  44.2 3.8 %collective-permute-start.6 = (f32[2,4,128]{2,1,0:T(4,128)S(1)}, f32[2,4,128]{2,1,0:T(4,128)S(1)}, u32[]{:S(2)}, u32[]{:S(2)}) collective-permute-start(f32[2,4,128]{2,1,0:T(4,128)S(1)} %get-tuple-element.39), channel_id=1, source_target_pairs={{0,2},{2,0},{1,3},{3,1},{4,6},{6,4},{5,7},{7,5},{8,10},{10,8},{9,1... | collective-permute-start | bytes 12296 | tf_op jit(solution)/shard_map/ppermute | solution.py:345
  44.3 4.5 %collective-permute-start.7 = (f32[2,4,128]{2,1,0:T(4,128)S(1)}, f32[2,4,128]{2,1,0:T(4,128)S(1)}, u32[]{:S(2)}, u32[]{:S(2)}) collective-permute-start(f32[2,4,128]{2,1,0:T(4,128)S(1)} %get-tuple-element.40), channel_id=1, source_target_pairs={{0,1},{1,0},{2,3},{3,2},{4,5},{5,4},{6,7},{7,6},{8,9},{9,8},{10,11... | collective-permute-start | bytes 12296 | tf_op jit(solution)/shard_map/ppermute | solution.py:346
  58.0 11.5 %collective-permute-start.8 = (f32[2,16,8,128]{3,2,1,0:T(8,128)S(1)}, f32[2,16,8,128]{3,2,1,0:T(8,128)S(1)}, u32[]{:S(2)}, u32[]{:S(2)}) collective-permute-start(f32[2,16,8,128]{3,2,1,0:T(8,128)S(1)} %get-tuple-element.41), channel_id=1, source_target_pairs={{0,4},{4,0},{8,12},{12,8},{16,20},{20,16},{24,28},{28,24},{32,36},... | collective-permute-start | bytes 393224 | tf_op jit(solution)/shard_map/ppermute | solution.py:343
  58.9 10.6 %collective-permute-start.9 = (f32[2,16,8,128]{3,2,1,0:T(8,128)S(1)}, f32[2,16,8,128]{3,2,1,0:T(8,128)S(1)}, u32[]{:S(2)}, u32[]{:S(2)}) collective-permute-start(f32[2,16,8,128]{3,2,1,0:T(8,128)S(1)} %get-tuple-element.42), channel_id=1, source_target_pairs={{0,0},{4,8},{8,4},{12,16},{16,12},{20,24},{24,20},{28,32},{32,28},... | collective-permute-start | bytes 393224 | tf_op jit(solution)/shard_map/ppermute | solution.py:344
  63.8 4.9 %collective-permute-start.10 = (f32[2,4,128]{2,1,0:T(4,128)S(1)}, f32[2,4,128]{2,1,0:T(4,128)S(1)}, u32[]{:S(2)}, u32[]{:S(2)}) collective-permute-start(f32[2,4,128]{2,1,0:T(4,128)S(1)} %get-tuple-element.43), channel_id=1, source_target_pairs={{0,2},{2,0},{1,3},{3,1},{4,6},{6,4},{5,7},{7,5},{8,10},{10,8},{9,1... | collective-permute-start | bytes 12296 | tf_op jit(solution)/shard_map/ppermute | solution.py:345
  63.9 5.6 %collective-permute-start.11 = (f32[2,4,128]{2,1,0:T(4,128)S(1)}, f32[2,4,128]{2,1,0:T(4,128)S(1)}, u32[]{:S(2)}, u32[]{:S(2)}) collective-permute-start(f32[2,4,128]{2,1,0:T(4,128)S(1)} %get-tuple-element.44), channel_id=1, source_target_pairs={{0,1},{1,0},{2,3},{3,2},{4,5},{5,4},{6,7},{7,6},{8,9},{9,8},{10,11... | collective-permute-start | bytes 12296 | tf_op jit(solution)/shard_map/ppermute | solution.py:346
  79.1 10.7 %collective-permute-start.15 = (f32[2,4,128]{2,1,0:T(4,128)S(1)}, f32[2,4,128]{2,1,0:T(4,128)S(1)}, u32[]{:S(2)}, u32[]{:S(2)}) collective-permute-start(f32[2,4,128]{2,1,0:T(4,128)S(1)} %get-tuple-element.49), channel_id=1, source_target_pairs={{0,1},{1,0},{2,3},{3,2},{4,5},{5,4},{6,7},{7,6},{8,9},{9,8},{10,11... | collective-permute-start | bytes 12296 | tf_op jit(solution)/shard_map/ppermute | solution.py:346
  83.7 6.0 %copy-start.5 = (f32[2,2,4,128]{3,2,1,0:T(4,128)S(1)}, f32[2,2,4,128]{3,2,1,0:T(4,128)}, u32[]{:S(2)}) copy-start(f32[2,2,4,128]{3,2,1,0:T(4,128)} %refs_12_.5) | copy-start | bytes 24580
  83.7 6.1 %collective-permute-start.14 = (f32[2,4,128]{2,1,0:T(4,128)S(1)}, f32[2,4,128]{2,1,0:T(4,128)S(1)}, u32[]{:S(2)}, u32[]{:S(2)}) collective-permute-start(f32[2,4,128]{2,1,0:T(4,128)S(1)} %get-tuple-element.48), channel_id=1, source_target_pairs={{0,2},{2,0},{1,3},{3,1},{4,6},{6,4},{5,7},{7,5},{8,10},{10,8},{9,1... | collective-permute-start | bytes 12296 | tf_op jit(solution)/shard_map/ppermute | solution.py:345
  83.8 7.2 %collective-permute-start.12 = (f32[2,128,128]{2,1,0:T(8,128)S(1)}, f32[2,128,128]{2,1,0:T(8,128)S(1)}, u32[]{:S(2)}, u32[]{:S(2)}) collective-permute-start(f32[2,128,128]{2,1,0:T(8,128)S(1)} %get-tuple-element.46), channel_id=1, source_target_pairs={{0,4},{4,0},{8,12},{12,8},{16,20},{20,16},{24,28},{28,24},{32,36},... | collective-permute-start | bytes 393224 | tf_op jit(solution)/shard_map/ppermute | solution.py:343
  83.9 11.5 %collective-permute-start.13 = (f32[2,128,128]{2,1,0:T(8,128)S(1)}, f32[2,128,128]{2,1,0:T(8,128)S(1)}, u32[]{:S(2)}, u32[]{:S(2)}) collective-permute-start(f32[2,128,128]{2,1,0:T(8,128)S(1)} %get-tuple-element.47), channel_id=1, source_target_pairs={{0,0},{4,8},{8,4},{12,16},{16,12},{20,24},{24,20},{28,32},{32,28},... | collective-permute-start | bytes 393224 | tf_op jit(solution)/shard_map/ppermute | solution.py:344
where the time goes:
time: 97.6 us; the launch traced here: 96.2 us
  starting transfers between devices  40.9 us (42%)
  Pallas kernels  37.1 us (38%)
  waiting for transfers between devices  9.85 us (10%)
  local copies, waits for them, and re-layouts  6.11 us (6%)
  between operations  1.46 us (1%)
    pallas_call x4, Pallas kernels, solve(): pl.pallas_call(functools.partial(kernel, first, final), out_shape=[jax.Sh...  37.1 us
    ppermute x4, starting transfers between devices, exchange(): lax.ppermute(out_b, 'gx', pairs_b)  20.2 us
    ppermute x4, starting transfers between devices, exchange(): lax.ppermute(out_z, 'gz', swap)  14.7 us
    ppermute x4, waiting for transfers between devices, exchange(): lax.ppermute(out_b, 'gx', pairs_b)  7.36 us
    unnamed x18, local copies, waits for them, and re-layouts  6.11 us
    ppermute x4, starting transfers between devices, exchange(): lax.ppermute(out_a, 'gx', pairs_a)  4.73 us
    ppermute x4, waiting for transfers between devices, exchange(): lax.ppermute(out_z, 'gz', swap)  2.1 us
  transfers between devices with their start and end apart: 16, of which 7 were waited for; matrix products, arithmetic and copies ran while one was open for 1% of the time, Pallas kernels for 0%

commit v1 on v0

v1 whole, which is shorter than its diff:
```python
import functools

import jax
import jax.numpy as jnp
from jax import lax
from jax.experimental import pallas as pl
from jax.experimental.pallas import tpu as pltpu
from jax.sharding import PartitionSpec as P

NT = 2
SWEEPS = 8
ITERS = 4
NMAT = 8
SPAN_X = 4
SPAN = 128
HALF = SPAN // 2
SUB = 8
TURN = 8

p_robin = 1.5
dt_coarse = 0.5
rho_bound = 0.9

RHO2 = rho_bound**2
SHIFT = 1.0 - RHO2
QUAD = RHO2 * RHO2 / 4.0 + SHIFT
Y_ONE = 2.0 / RHO2 - 1.0
GAIN = 128.0 / (RHO2**4 * (8.0 * Y_ONE**4 - 8.0 * Y_ONE**2 + 1.0))

F32 = jnp.float32
TILES = [(x, z) for x in range(SPAN_X) for z in range(2)]
ROWS = TURN * len(TILES) * SUB
ROWS_X = TURN * (SPAN_X - 1) * 2 * SUB
ROWS_A = TURN * 2 * SUB


def at(j, x, z):
    return pl.ds(((j * SPAN_X + x) * 2 + z) * SUB, SUB)


def at_x(j, x, z):
    return pl.ds(((j * (SPAN_X - 1) + x) * 2 + z) * SUB, SUB)


def at_face(n, j, z):
    return pl.ds(pl.multiple_of(((n * TURN + j) * 2 + z) * SUB, SUB), SUB)


def aligned(rows):
    return pl.ds(pl.multiple_of(rows, SUB), SUB)


def lanes():
    return lax.broadcasted_iota(jnp.int32, (SUB, SPAN), 1)


def sublanes():
    return lax.broadcasted_iota(jnp.int32, (SUB, SPAN), 0)


def harmonic(left_k, right_k):
    return 2.0 * left_k * right_k / (left_k + right_k)


def pick(bits, table_ref):
    level = [table_ref[i] for i in range(NMAT)]
    for bit in bits:
        level = [jnp.where(bit, level[2 * i + 1], level[2 * i]) for i in range(len(level) // 2)]
    return level[0]


def up_z(value):
    return pltpu.roll(value, SPAN - 1, 1)


def down_z(value):
    return pltpu.roll(value, 1, 1)


def other_half(value):
    return pltpu.roll(value, HALF, 1)


def up_y(value):
    turned = pltpu.roll(value, SUB - 1, 0)
    return jnp.where(sublanes() < SUB - 1, turned, other_half(turned))


def down_y(value):
    turned = pltpu.roll(value, 1, 0)
    return jnp.where(sublanes() > 0, turned, other_half(turned))


def pairing(back):
    row = lax.broadcasted_iota(jnp.int32, (2 * SPAN, 2 * SPAN), 1 if back else 0)
    col = lax.broadcasted_iota(jnp.int32, (2 * SPAN, 2 * SPAN), 0 if back else 1)
    half, z = row // SPAN, row % SPAN
    place = (z % 2) * SPAN + half * HALF + z // 2
    return jnp.where(col == place, 1.0, 0.0).astype(jnp.bfloat16)


def moved(value, matrix, narrow=False):
    dot = functools.partial(jnp.dot, preferred_element_type=F32)
    high = value.astype(jnp.bfloat16)
    if narrow:
        return dot(high, matrix)
    rest = value - high.astype(F32)
    middle = rest.astype(jnp.bfloat16)
    low = (rest - middle.astype(F32)).astype(jnp.bfloat16)
    return dot(high, matrix) + (dot(middle, matrix) + dot(low, matrix))


def rows_of(j, half):
    return pl.ds(HALF * half + j, SUB, stride=TURN)


def split(planes, matrix, narrow=False):
    pieces = []
    for ref, lead in planes:
        for j in range(TURN):
            halves = [ref[(*lead, rows_of(j, half), slice(None))].astype(F32) for half in range(2)]
            pieces.append(jnp.concatenate(halves, 1))
    out = moved(jnp.concatenate(pieces, 0), matrix, narrow)

    def tile(plane, j, z):
        row = (plane * TURN + j) * SUB
        return out[row : row + SUB, z * SPAN : (z + 1) * SPAN]

    return tile


def join(planes, matrix):
    pieces = [jnp.concatenate(tiles[j], 1) for _, _, tiles in planes for j in range(TURN)]
    out = moved(jnp.concatenate(pieces, 0), matrix)
    for plane, (ref, lead, _) in enumerate(planes):
        for j in range(TURN):
            row = (plane * TURN + j) * SUB
            for half in range(2):
                ref[(*lead, rows_of(j, half), slice(None))] = out[row : row + SUB, half * SPAN : (half + 1) * SPAN]


def prepare(steps, matrix, arrive, initial, material, conduct, capacity, cx, cy, cw, cz, weight, scale, start, kcell):
    lane, sub = lanes(), sublanes()
    inverse_h = steps.astype(F32) * (1.0 / dt_coarse)
    tiles = split([(material, (x,)) for x in range(SPAN_X)], matrix, narrow=True)
    for j in range(TURN):
        for x in range(SPAN_X):
            for z in range(2):
                mat = tiles(x, j, z).astype(jnp.int32)
                bits = [(mat & 1) != 0, (mat & 2) != 0, (mat & 4) != 0]
                kcell[at(j, x, z), :] = pick(bits, conduct)
                start[at(j, x, z), :] = pick(bits, capacity)
    inner = (lane != HALF - 1) & (lane != SPAN - 1)
    for j in range(TURN):
        for x, z in TILES:
            here = kcell[at(j, x, z), :]
            if x < SPAN_X - 1:
                cx[at_x(j, x, z), :] = harmonic(here, kcell[at(j, x + 1, z), :])
            if j < TURN - 1:
                cy[at(j, x, z), :] = harmonic(here, kcell[at(j + 1, x, z), :])
            else:
                link = harmonic(here, up_y(kcell[at(0, x, z), :]))
                cy[at(j, x, z), :] = jnp.where((sub == SUB - 1) & (lane >= HALF), 0.0, link)
            if z == 0:
                cz[at(j, x, z), :] = harmonic(here, kcell[at(j, x, 1), :])
            else:
                cz[at(j, x, z), :] = jnp.where(inner, harmonic(here, up_z(kcell[at(j, x, 0), :])), 0.0)
    for j in range(TURN):
        for x, z in TILES:
            base = cz[at(j, x, 0), :] + (cz[at(j, x, 1), :] if z else down_z(cz[at(j, x, 1), :]))
            base = base + cy[at(j, x, z), :]
            base = base + (cy[at(j - 1, x, z), :] if j > 0 else down_y(cy[at(TURN - 1, x, z), :]))
            if x < SPAN_X - 1:
                base = base + cx[at_x(j, x, z), :]
            if x > 0:
                base = base + cx[at_x(j, x - 1, z), :]
            if x in (0, SPAN_X - 1):
                base = base + p_robin
            end = HALF - 1 if z else 0
            base = base + jnp.where((lane == end) | (lane == end + HALF), p_robin, 0.0)
            if j == 0:
                base = base + jnp.where((sub == 0) & (lane < HALF), p_robin, 0.0)
            if j == TURN - 1:
                base = base + jnp.where((sub == SUB - 1) & (lane >= HALF), p_robin, 0.0)
            diagonal = start[at(j, x, z), :] * inverse_h + base
            root = lax.rsqrt(diagonal)
            root = root * (1.5 - 0.5 * diagonal * root * root)
            scale[at(j, x, z), :] = root
            weight[at(j, x, z), :] = -base * root * root
            start[at(j, x, z), :] = diagonal * root
    for j in range(TURN):
        for x, z in TILES:
            here = scale[at(j, x, z), :]
            if x < SPAN_X - 1:
                cx[at_x(j, x, z), :] = cx[at_x(j, x, z), :] * here * scale[at(j, x + 1, z), :]
            after = scale[at(j + 1, x, z), :] if j < TURN - 1 else up_y(scale[at(0, x, z), :])
            cy[at(j, x, z), :] = cy[at(j, x, z), :] * here * after
            beside = up_z(scale[at(j, x, 0), :]) if z else scale[at(j, x, 1), :]
            cz[at(j, x, z), :] = cz[at(j, x, z), :] * here * beside
    for x, z in TILES:
        cw[at(0, x, z), :] = down_y(cy[at(TURN - 1, x, z), :])
    arrive(1)
    tiles = split([(initial, (x,)) for x in range(SPAN_X)], matrix)
    for j in range(TURN):
        for x, z in TILES:
            start[at(j, x, z), :] = start[at(j, x, z), :] * tiles(x, j, z)


def couple(cx, cy, cw, cz, begin, source, emit):
    def load(j):
        return {p: source[at(j, *p), :] for p in TILES}

    def wrap_down(row):
        return {p: cw[at(0, *p), :] * down_y(row[p]) for p in TILES}

    here = load(begin)
    before = load((begin - 1) % TURN)
    if begin == 0:
        before = wrap_down(before)
    else:
        before = {p: cy[at(begin - 1, *p), :] * before[p] for p in TILES}
    for turn in range(TURN):
        j = (begin + turn) % TURN
        following = load((j + 1) % TURN)
        after = following if j < TURN - 1 else {p: up_y(following[p]) for p in TILES}
        total, later = {}, {}
        for p in TILES:
            link = cy[at(j, *p), :]
            total[p] = before[p] + link * after[p]
            if j < TURN - 1:
                later[p] = link * here[p]
        for x in range(SPAN_X):
            even, odd = (x, 0), (x, 1)
            link = cz[at(j, *even), :]
            total[even] = total[even] + link * here[odd]
            total[odd] = total[odd] + link * here[even]
            link = cz[at(j, *odd), :]
            total[odd] = total[odd] + link * up_z(here[even])
            total[even] = total[even] + down_z(link * here[odd])
        for x in range(SPAN_X - 1):
            for z in range(2):
                link = cx[at_x(j, x, z), :]
                total[(x, z)] = total[(x, z)] + link * here[(x + 1, z)]
                total[(x + 1, z)] = total[(x + 1, z)] + link * here[(x, z)]
        emit(j, here, total)
        before = later if j < TURN - 1 else wrap_down(here)
        here = following


def kernel(first, final, *refs):
    refs = list(refs)
    take = lambda n: [refs.pop(0) for _ in range(n)]
    if first:
        far = take(8)
        cx, cy, cw, cz, weight, scale, start, keep_x, keep_y, keep_z = take(10)
    else:
        (substeps,) = take(1)
        cx, cy, cw, cz, weight, scale, start, keep_x, keep_y, keep_z = take(10)
        face_low, face_high, come_y, come_z = take(4)
    if final:
        (field_out,) = take(1)
    out_low, out_high, out_y, out_z = take(4)
    if first:
        kcell, face_low, face_high, come_y, come_z = take(5)
        near = take(8)
        (arrivals,) = take(1)
    field, old, load, res, one, two, three = take(7)
    near_links, far_links = take(4), (cx, cy, cz, weight)
    if not first:
        for source, target in zip(far_links, near_links):
            target[...] = source[...]
    cx, cy, cz, weight = near_links
    lines, spare, turned_z, cols_z, sum_z = take(5)

    place_x, place_y, place_z = (lax.axis_index("gx"), lax.axis_index("gy"), lax.axis_index("gz"))
    ends_x = (place_x == 0, place_x == lax.axis_size("gx") - 1)
    lane, sub = lanes(), sublanes()

    if first:
        order = (2, 3, 4, 1, 0, 5, 6, 7)
        copies = {i: pltpu.make_async_copy(far[i], near[i], arrivals.at[i]) for i in order}
        for i in order:
            copies[i].start()
        initial, material, conduct, capacity, substeps, trace_x, trace_y, trace_z = near
        matrix = pairing(False)
        for i in (2, 3, 4, 1):
            copies[i].wait()
        steps = substeps[0]
        prepare(
            steps, matrix, lambda _: copies[0].wait(),
            initial, material, conduct, capacity, cx, cy, cw, cz, weight, scale, start, kcell,
        )
        for source, target in zip(near_links, far_links):
            target[...] = source[...]
        for i in (5, 6, 7):
            copies[i].wait()
        low_tiles, high_tiles = [split([(trace_x, (side, n)) for n in range(NT)], matrix) for side in range(2)]
        for n in range(NT):
            for j in range(TURN):
                for z in range(2):
                    tile = at_face(n, j, z)
                    face_low[tile, :] = low_tiles(n, j, z)
                    face_high[tile, :] = high_tiles(n, j, z)
                    keep_x[tile, :] = jnp.where(ends_x[0], low_tiles(n, j, z), high_tiles(n, j, z))
        for n in range(NT):
            for x in range(SPAN_X):
                keep_z[n, pl.ds(x, 1), :] = trace_z[n, place_z, pl.ds(x, 1), :]
                come_z[n, pl.ds(x, 1), :] = trace_z[n, 1 - place_z, pl.ds(x, 1), :]
                for side in range(2):
                    spare[pl.ds(SUB * side + SPAN_X * n + x, 1), :] = trace_y[n, x, pl.ds(side, 1), :]
        both = spare[pl.ds(0, 2 * SUB), :]
        both = moved(jnp.concatenate([both, both], 1), matrix)
        for z in range(2):
            spare[pl.ds(2 * SUB * (z + 1), 2 * SUB), :] = both[:, z * SPAN : (z + 1) * SPAN]
        for n in range(NT):
            for i, (x, z) in enumerate(TILES):
                row = SPAN_X * n + x + 2 * SUB * (z + 1)
                keep_y[pl.ds(SUB * n + i, 1), :] = spare[pl.ds(row + SUB * place_y, 1), :]
                come_y[pl.ds(SUB * n + i, 1), :] = spare[pl.ds(row + SUB * (1 - place_y), 1), :]
    else:
        steps = substeps[0]
    last_part = jnp.where(steps == 2, F32(p_robin), F32(2.0 * p_robin))
    mid_part = jnp.where(steps == 2, F32(p_robin), F32(0.0))
    faces_x = ((0, face_low, out_low), (SPAN_X - 1, face_high, out_high))

    turned_z[...] = jnp.zeros((SPAN, SPAN), F32)
    inner_z = 1 - place_z
    for n in range(NT):
        for x in range(SPAN_X):
            row = 2 * (SPAN_X * n + x)
            for side, data in ((inner_z, come_z), (place_z, keep_z)):
                line = data[n, pl.ds(x, 1), :]
                place = row + (HALF - 1) * side
                turned_z[pl.ds(place, 1), :] = line
                turned_z[pl.ds((place + HALF) % SPAN, 1), :] = line
    cols_z[...] = turned_z[...].T
    outer_lanes = (lane < HALF // 2) | (lane >= SPAN - HALF // 2)
    low_half = outer_lanes == (lane % 2 == 0)
    for j in range(TURN):
        value = jnp.where(low_half, cols_z[rows_of(j, 0), :], cols_z[rows_of(j, 1), :])
        turned_z[pl.ds(SUB * j, SUB), :] = value
        sum_z[pl.ds(SUB * j, SUB), :] = jnp.zeros((SUB, SPAN), F32)
    for j in range(TURN):
        for p in TILES:
            value = start[at(j, *p), :]
            field[at(j, *p), :] = value
    end_even = (lane == 0) | (lane == HALF)
    end_odd = (lane == HALF - 1) | (lane == SPAN - 1)
    corner_low = (sub == 0) & (lane < HALF)
    corner_high = (sub == SUB - 1) & (lane >= HALF)

    if final:
        back = pairing(True)

    def coarse(n, nothing):
        tile_y = aligned(SUB * n)
        kept, come = keep_y[tile_y, :], come_y[tile_y, :]
        lines[pl.ds(0, SUB), :] = jnp.where(place_y == 0, kept, come)
        lines[pl.ds(SUB, SUB), :] = jnp.where(place_y == 0, come, kept)
        for j in range(TURN):
            column = turned_z[pl.ds(SUB * j, SUB), :]
            for x in range(SPAN_X):
                around = pltpu.roll(column, (SPAN - 2 * x - 2 * SPAN_X * n) % SPAN, 1)
                for z, ends in enumerate((end_even, end_odd)):
                    value = jnp.where(ends, around, 0.0)
                    line = 2 * x + z
                    if j == 0:
                        value = value + jnp.where(corner_low, lines[pl.ds(line, 1), :], 0.0)
                    if j == TURN - 1:
                        value = value + jnp.where(corner_high, lines[pl.ds(SUB + line, 1), :], 0.0)
                    load[at(j, x, z), :] = value * scale[at(j, x, z), :]
        for j in range(TURN):
            for z in range(2):
                tile = at_face(n, j, z)
                for end, (x, data, _) in zip(ends_x, faces_x):
                    value = jnp.where(end, keep_x[tile, :], data[tile, :])
                    load[at(j, x, z), :] = load[at(j, x, z), :] + value * scale[at(j, x, z), :]

        def substep(index, nothing):
            def to_res(j, here, total):
                for p in TILES:
                    tile = at(j, *p)
                    old[tile, :] = here[p]
                    res[tile, :] = total[p] + weight[tile, :] * here[p] + load[tile, :]

            def to_one(j, here, total):
                for p in TILES:
                    one[at(j, *p), :] = total[p] + here[p]

            def plain(out):
                def emit(j, here, total):
                    for p in TILES:
                        out[at(j, *p), :] = total[p]

                return emit

            def mixed(out, other, factor):
                def emit(j, here, total):
                    for p in TILES:
                        tile = at(j, *p)
                        out[tile, :] = total[p] + factor * other[tile, :]

                return emit

            def close(j, here, total):
                for p in TILES:
                    tile = at(j, *p)
                    field[tile, :] = old[tile, :] + GAIN * (total[p] + QUAD * res[tile, :])

            go = functools.partial(couple, cx, cy, cw, cz)
            go(0, field, to_res)
            go(1, res, to_one)
            go(2, one, plain(two))
            go(3, two, mixed(res, one, SHIFT))
            go(4, res, plain(one))
            go(5, one, mixed(two, res, -RHO2))
            go(6, two, plain(three))
            go(7, three, close)
            return nothing

        lax.fori_loop(0, steps, substep, 0)

        def mean(start_row, last, mid, step=1):
            if step == 1:
                rows = aligned(start_row)
            else:
                rows = pl.ds(start_row, SUB, stride=step)
            return scale[rows, :] * (last * field[rows, :] + mid * old[rows, :])

        planes = []
        for x, data, out in faces_x:
            made = []
            for j in range(TURN):
                pair = []
                for z in range(2):
                    tile = at_face(n, j, z)
                    pair.append(mean(at(j, x, z).start, last_part, mid_part) - data[tile, :])
                    if not final:
                        out[tile, :] = pair[z]
                made.append(pair)
            planes.append((out, (n,), made))
        if final:
            join(planes, back)
        for j in range(TURN):
            gathered = sum_z[pl.ds(SUB * j, SUB), :]
            for x in range(SPAN_X):
                value = mean(at(j, x, 0).start + SUB * inner_z, last_part, mid_part)
                shift = 2 * x + 2 * SPAN_X * n
                mine = (lane - (HALF - 1) * inner_z - shift) % HALF == 0
                gathered = gathered + jnp.where(mine, pltpu.roll(value, shift, 1), 0.0)
            sum_z[pl.ds(SUB * j, SUB), :] = gathered
        corner = jnp.where(place_y == 0, at(TURN - 1, 0, 0).start + SUB - 1, 0)
        value = mean(corner, last_part, mid_part, SUB) - come_y[tile_y, :]
        if final:
            value = jnp.where((lane >= HALF) == (place_y == 0), value, other_half(value))
            spare[tile_y, :] = value
        else:
            out_y[tile_y, :] = other_half(value)
        return nothing

    lax.fori_loop(0, NT, coarse, 0)

    for j in range(TURN):
        value = sum_z[pl.ds(SUB * j, SUB), :]
        for half in range(2):
            turned_z[rows_of(j, half), :] = value
    cols_z[...] = turned_z[...].T
    line_lane = lax.broadcasted_iota(jnp.int32, (1, SPAN), 1)
    for n in range(NT):
        for x in range(SPAN_X):
            place = 2 * (SPAN_X * n + x) + (HALF - 1) * inner_z
            low, high = cols_z[pl.ds(place, 1), :], cols_z[pl.ds((place + HALF) % SPAN, 1), :]
            out_z[n, pl.ds(x, 1), :] = jnp.where(line_lane < HALF, low, high) - come_z[n, pl.ds(x, 1), :]
    if final:
        even, odd_z = spare[pl.ds(0, SUB, stride=2), :], spare[pl.ds(1, SUB, stride=2), :]
        both = jnp.concatenate([even, odd_z], 1)
        spare[pl.ds(2 * SUB, 2 * SUB), :] = moved(jnp.concatenate([both, both], 0), back)[:, :SPAN]
        for n in range(NT):
            for x in range(SPAN_X):
                out_y[n, pl.ds(x, 1), :] = spare[pl.ds(2 * SUB + SPAN_X * n + x, 1), :]
        planes = []
        for x in range(SPAN_X):
            made = [[field[at(j, x, z), :] * scale[at(j, x, z), :] for z in range(2)] for j in range(TURN)]
            planes.append((field_out, (x,), made))
        join(planes, back)


def solve(first, final, *operands):
    vmem = pl.BlockSpec(memory_space=pltpu.VMEM)
    smem = pl.BlockSpec(memory_space=pltpu.SMEM)
    far = pl.BlockSpec(memory_space=pltpu.MemorySpace.HBM)
    wide = lambda rows: (rows, SPAN)
    lines_z = (NT, SPAN_X, SPAN)
    if first:
        in_specs = [far] * 8
    else:
        in_specs = [smem] + [vmem] * 14
    shapes = []
    if first:
        shapes += [wide(ROWS_X), wide(ROWS), wide(len(TILES) * SUB)] + [wide(ROWS)] * 4
        shapes += [wide(NT * ROWS_A), wide(NT * SUB), lines_z]
    if final:
        shapes += [(SPAN_X, SPAN, SPAN)]
    shapes += [(NT, SPAN, SPAN) if final else wide(NT * ROWS_A)] * 2
    shapes += [lines_z if final else wide(NT * SUB), lines_z]
    scratch = []
    if first:
        scratch += [pltpu.VMEM(wide(ROWS), F32)] + [pltpu.VMEM(wide(NT * ROWS_A), F32)] * 2
        scratch += [pltpu.VMEM(wide(NT * SUB), F32), pltpu.VMEM(lines_z, F32)]
        for i, operand in enumerate(operands):
            space = pltpu.SMEM if i in (2, 3, 4) else pltpu.VMEM
            scratch.append(space(operand.shape, operand.dtype))
        scratch.append(pltpu.SemaphoreType.DMA((8,)))
    scratch += [pltpu.VMEM(wide(ROWS), F32)] * 7
    scratch += [pltpu.VMEM(wide(ROWS_X), F32)] + [pltpu.VMEM(wide(ROWS), F32)] * 3
    scratch += [pltpu.VMEM(wide(2 * SUB), F32), pltpu.VMEM(wide(6 * SUB), F32)]
    scratch += [pltpu.VMEM(wide(SPAN), F32)] * 2 + [pltpu.VMEM(wide(TURN * SUB), F32)]
    return pl.pallas_call(
        functools.partial(kernel, first, final),
        out_shape=[jax.ShapeDtypeStruct(shape, F32) for shape in shapes],
        in_specs=in_specs,
        out_specs=[vmem] * len(shapes),
        scratch_shapes=scratch,
        compiler_params=pltpu.CompilerParams(vmem_limit_bytes=(52 if first else 24) * 1024 * 1024),
    )(*operands)


def exchange(out_low, out_high, out_y, out_z):
    count = lax.axis_size("gx")
    up = [(i, (i + 1) % count) for i in range(count)]
    down = [(j, i) for i, j in up]
    swap = [(0, 1), (1, 0)]
    return (
        lax.ppermute(out_high, "gx", up),
        lax.ppermute(out_low, "gx", down),
        lax.ppermute(out_y, "gy", swap),
        lax.ppermute(out_z, "gz", swap),
    )


def local(initial, material, conduct, capacity, substeps, trace_x, trace_y, trace_z):
    steps = substeps.reshape(1)
    place_x, place_y, place_z = (lax.axis_index("gx"), lax.axis_index("gy"), lax.axis_index("gz"))
    results = solve(True, False, initial, material, conduct, capacity, steps, trace_x, trace_y, trace_z)
    prepared, sent = results[:10], results[10:]
    for iteration in range(1, ITERS):
        arrived = exchange(*sent)
        final = iteration == ITERS - 1
        sent = solve(False, final, steps, *prepared, *arrived)
    field, *sent = sent
    face_low, face_high, come_y, come_z = exchange(*sent)
    face_low = jnp.where(place_x == 0, trace_x[0], face_low)
    face_high = jnp.where(place_x == lax.axis_size("gx") - 1, trace_x[1], face_high)
    got_x = jnp.stack([face_low, face_high], 0)
    got_y = jnp.stack([jnp.where(place_y == side, trace_y[:, :, side], come_y) for side in range(2)], 2)
    got_z = jnp.stack([jnp.where(place_z == side, trace_z[:, side], come_z) for side in range(2)], 1)
    return (field, got_x, got_y, got_z)


def solution(mesh):
    placed = (
        P("gx", "gy", "gz"),
        P("gx", "gy", "gz"),
        P(),
        P(),
        P("gx", "gy", "gz"),
        P("gx", None, "gy", "gz"),
        P(None, "gx", "gy", "gz"),
        P(None, "gz", "gx", "gy"),
    )
    return jax.shard_map(
        local,
        mesh=mesh,
        in_specs=placed,
        out_specs=(
            P("gx", "gy", "gz"),
            P("gx", None, "gy", "gz"),
            P(None, "gx", "gy", "gz"),
            P(None, "gz", "gx", "gy"),
        ),
        check_vma=False,
    )
```

time: 97.6 us -> 76.4 us (0.78)
  the two profiles are of different devices: /device:TPU:3 before, /device:TPU:1 now
where the time goes in v1:
time: 76.4 us; the launch traced here: 76.2 us
  starting transfers between devices  49.7 us (65%)
  Pallas kernels  15 us (20%)
  waiting for transfers between devices  6.04 us (8%)
  local copies, waits for them, and re-layouts  3.27 us (4%)
  between operations  1.42 us (2%)
  other arithmetic  0.78 us (1%)
    ppermute x4, starting transfers between devices, exchange(): lax.ppermute(out_low, 'gx', down)  31.9 us
    pallas_call x4, Pallas kernels, solve(): pl.pallas_call(functools.partial(kernel, first, final), out_shape=[jax.Sh...  15 us
    ppermute x4, starting transfers between devices, exchange(): lax.ppermute(out_z, 'gz', swap)  9.92 us
    ppermute x4, starting transfers between devices, exchange(): lax.ppermute(out_high, 'gx', up)  4.72 us
    ppermute x4, waiting for transfers between devices, exchange(): lax.ppermute(out_high, 'gx', up)  3.4 us
    unnamed x14, local copies, waits for them, and re-layouts  3.27 us
    ppermute x4, starting transfers between devices, exchange(): lax.ppermute(out_y, 'gy', swap)  3.15 us
    ppermute x4, waiting for transfers between devices, exchange(): lax.ppermute(out_z, 'gz', swap)  2.47 us
  transfers between devices with their start and end apart: 16, of which 6 were waited for; matrix products, arithmetic and copies ran while one was open for 2% of the time, Pallas kernels for 0%

profile of v1, /device:TPU:1, one launch (start us, length us, event | category | flops | bytes accessed | tf_op | source)
XLA Modules:
  0.0 76.2 jit_solution(12817595114900706145)
XLA Ops:
  1.3 0.0 copy-start.3
  1.3 0.0 copy-start.4
  1.3 0.6 copy-done.3
  1.9 0.0 copy-done.4
  2.0 0.0 copy-start
  2.0 0.7 copy-done
  2.6 0.0 copy-start.1
  2.7 0.7 copy-done.1
  3.3 5.2 %shard_map.111 = (f32[384,128]{1,0:T(8,128)S(1)}, f32[512,128]{1,0:T(8,128)S(1)}, f32[64,128]{1,0:T(8,128)S(1)}, f32[512,128]{1,0:T(8,128)S(1)}, f32[512,128]{1,...) custom-call(f32[4,128,128]{2,1,0:T(8,128)} %refs_0_.1, ...), custom_call_target="tpu_custom_call" | custom-call | tf_op jit(solution)/shard_map/pallas_call | solution.py:518
  8.6 4.5 %collective-permute-start = (f32[256,128]{1,0:T(8,128)S(1)}, f32[256,128]{1,0:T(8,128)S(1)}, u32[]{:S(2)}, u32[]{:S(2)}) collective-permute-start(f32[256,128]{1,0:T(8,128)S(1)} %get-tuple-element.41), channel_id=1, source_target_pairs={{0,4},{4,8},{8,12},{12,16},{16,20},{20,24},{24,28},{28,32},{32,36}... | collective-permute-start | bytes 393224 | tf_op jit(solution)/shard_map/ppermute | solution.py:534
  13.1 6.9 %collective-permute-start.1 = (f32[256,128]{1,0:T(8,128)S(1)}, f32[256,128]{1,0:T(8,128)S(1)}, u32[]{:S(2)}, u32[]{:S(2)}) collective-permute-start(f32[256,128]{1,0:T(8,128)S(1)} %get-tuple-element.42), channel_id=1, source_target_pairs={{4,0},{8,4},{12,8},{16,12},{20,16},{24,20},{28,24},{32,28},{36,32}... | collective-permute-start | bytes 393224 | tf_op jit(solution)/shard_map/ppermute | solution.py:535
  19.9 0.7 collective-permute-start.2
  20.7 1.2 %collective-permute-start.3 = (f32[2,4,128]{2,1,0:T(4,128)S(1)}, f32[2,4,128]{2,1,0:T(4,128)S(1)}, u32[]{:S(2)}, u32[]{:S(2)}) collective-permute-start(f32[2,4,128]{2,1,0:T(4,128)S(1)} %get-tuple-element.44), channel_id=1, source_target_pairs={{0,1},{1,0},{2,3},{3,2},{4,5},{5,4},{6,7},{7,6},{8,9},{9,8},{10,11... | collective-permute-start | bytes 12296 | tf_op jit(solution)/shard_map/ppermute | solution.py:537
  21.9 0.8 %collective-permute-done.3.refs_14_ = f32[2,4,128]{2,1,0:T(4,128)S(1)} collective-permute-done((f32[2,4,128]{2,1,0:T(4,128)S(1)}, f32[2,4,128]{2,1,0:T(4,128)S(1)}, u32[]{:S(2)}, u32[]{:S(2)}) %collective-permute-start.3) | collective-permute-done | bytes 4128 | tf_op jit(solution)/shard_map/ppermute | solution.py:537
  22.8 0.1 collective-permute-done.2.refs_13_
  22.9 1.0 %collective-permute-done.refs_11_ = f32[256,128]{1,0:T(8,128)S(1)} collective-permute-done((f32[256,128]{1,0:T(8,128)S(1)}, f32[256,128]{1,0:T(8,128)S(1)}, u32[]{:S(2)}, u32[]{:S(2)}) %collective-permute-start) | collective-permute-done | bytes 131104 | tf_op jit(solution)/shard_map/ppermute | solution.py:534
  23.9 0.0 collective-permute-done.1.refs_12_
  23.9 2.9 %shard_map.112 = (f32[256,128]{1,0:T(8,128)S(1)}, f32[256,128]{1,0:T(8,128)S(1)}, f32[16,128]{1,0:T(8,128)S(1)}, f32[2,4,128]{2,1,0:T(4,128)S(1)}) custom-call(s32[1]{0:T(128)} %bitcast.40.refs_0_, f32[384,128]{1,0:T(8,128)S(1)} %get-tuple-element.31.refs_1_, f32[512,128]{1,0:T(8,128)S(1)} %get-tuple-element.32.refs_2_, ...), custom_call_target="tpu_custom_call" | custom-call | tf_op jit(solution)/shard_map/pallas_call | solution.py:518
  26.8 0.1 collective-permute-start.4
  26.9 9.2 %collective-permute-start.5 = (f32[256,128]{1,0:T(8,128)S(1)}, f32[256,128]{1,0:T(8,128)S(1)}, u32[]{:S(2)}, u32[]{:S(2)}) collective-permute-start(f32[256,128]{1,0:T(8,128)S(1)} %get-tuple-element.46), channel_id=1, source_target_pairs={{4,0},{8,4},{12,8},{16,12},{20,16},{24,20},{28,24},{32,28},{36,32}... | collective-permute-start | bytes 393224 | tf_op jit(solution)/shard_map/ppermute | solution.py:535
  36.1 0.0 collective-permute-start.6
  36.1 2.2 %collective-permute-start.7 = (f32[2,4,128]{2,1,0:T(4,128)S(1)}, f32[2,4,128]{2,1,0:T(4,128)S(1)}, u32[]{:S(2)}, u32[]{:S(2)}) collective-permute-start(f32[2,4,128]{2,1,0:T(4,128)S(1)} %get-tuple-element.48), channel_id=1, source_target_pairs={{0,1},{1,0},{2,3},{3,2},{4,5},{5,4},{6,7},{7,6},{8,9},{9,8},{10,11... | collective-permute-start | bytes 12296 | tf_op jit(solution)/shard_map/ppermute | solution.py:537
  38.2 0.8 %collective-permute-done.7.refs_14_ = f32[2,4,128]{2,1,0:T(4,128)S(1)} collective-permute-done((f32[2,4,128]{2,1,0:T(4,128)S(1)}, f32[2,4,128]{2,1,0:T(4,128)S(1)}, u32[]{:S(2)}, u32[]{:S(2)}) %collective-permute-start.7) | collective-permute-done | bytes 4128 | tf_op jit(solution)/shard_map/ppermute | solution.py:537
  39.1 0.0 collective-permute-done.6.refs_13_
  39.1 0.0 collective-permute-done.4.refs_11_
  39.1 0.0 collective-permute-done.5.refs_12_
  39.1 2.9 %shard_map.113 = (f32[256,128]{1,0:T(8,128)S(1)}, f32[256,128]{1,0:T(8,128)S(1)}, f32[16,128]{1,0:T(8,128)S(1)}, f32[2,4,128]{2,1,0:T(4,128)S(1)}) custom-call(s32[1]{0:T(128)} %bitcast.41.refs_0_, f32[384,128]{1,0:T(8,128)S(1)} %get-tuple-element.31.refs_1_, f32[512,128]{1,0:T(8,128)S(1)} %get-tuple-element.32.refs_2_, ...), custom_call_target="tpu_custom_call" | custom-call | tf_op jit(solution)/shard_map/pallas_call | solution.py:518
  42.0 0.1 collective-permute-start.8
  42.0 8.7 %collective-permute-start.9 = (f32[256,128]{1,0:T(8,128)S(1)}, f32[256,128]{1,0:T(8,128)S(1)}, u32[]{:S(2)}, u32[]{:S(2)}) collective-permute-start(f32[256,128]{1,0:T(8,128)S(1)} %get-tuple-element.50), channel_id=1, source_target_pairs={{4,0},{8,4},{12,8},{16,12},{20,16},{24,20},{28,24},{32,28},{36,32}... | collective-permute-start | bytes 393224 | tf_op jit(solution)/shard_map/ppermute | solution.py:535
  50.7 2.3 %collective-permute-start.10 = (f32[16,128]{1,0:T(8,128)S(1)}, f32[16,128]{1,0:T(8,128)S(1)}, u32[]{:S(2)}, u32[]{:S(2)}) collective-permute-start(f32[16,128]{1,0:T(8,128)S(1)} %get-tuple-element.51), channel_id=1, source_target_pairs={{0,2},{2,0},{1,3},{3,1},{4,6},{6,4},{5,7},{7,5},{8,10},{10,8},{9,1... | collective-permute-start | bytes 24584 | tf_op jit(solution)/shard_map/ppermute | solution.py:536
  53.0 1.6 %collective-permute-start.11 = (f32[2,4,128]{2,1,0:T(4,128)S(1)}, f32[2,4,128]{2,1,0:T(4,128)S(1)}, u32[]{:S(2)}, u32[]{:S(2)}) collective-permute-start(f32[2,4,128]{2,1,0:T(4,128)S(1)} %get-tuple-element.52), channel_id=1, source_target_pairs={{0,1},{1,0},{2,3},{3,2},{4,5},{5,4},{6,7},{7,6},{8,9},{9,8},{10,11... | collective-permute-start | bytes 12296 | tf_op jit(solution)/shard_map/ppermute | solution.py:537
  54.7 0.8 %collective-permute-done.11.refs_14_ = f32[2,4,128]{2,1,0:T(4,128)S(1)} collective-permute-done((f32[2,4,128]{2,1,0:T(4,128)S(1)}, f32[2,4,128]{2,1,0:T(4,128)S(1)}, u32[]{:S(2)}, u32[]{:S(2)}) %collective-permute-start.11) | collective-permute-done | bytes 4128 | tf_op jit(solution)/shard_map/ppermute | solution.py:537
  55.5 0.0 collective-permute-done.10.refs_13_
  55.5 0.0 collective-permute-done.8.refs_11_
  55.5 0.0 collective-permute-done.9.refs_12_
  55.5 0.0 copy-start.5
  55.5 4.0 %shard_map.114 = (f32[4,128,128]{2,1,0:T(8,128)}, f32[2,128,128]{2,1,0:T(8,128)S(1)}, f32[2,128,128]{2,1,0:T(8,128)S(1)}, f32[2,4,128]{2,1,0:T(4,128)S(1)}, f32[2,4,128]{2,1,0:T(4,128)S(1)}) custom-call(s32[1]{0:T(128)} %bitcast.42.refs_0_, f32[384,128]{1,0:T(8,128)S(1)} %get-tuple-element.31.refs_1_, f32[512,128]{1,0:T(8,128)S(1)} %get-tuple-element.32.refs_2_, ...), custom_call_target="tpu_custom_call" | custom-call | tf_op jit(solution)/shard_map/pallas_call | solution.py:518
  59.6 4.9 %collective-permute-start.15 = (f32[2,4,128]{2,1,0:T(4,128)S(1)}, f32[2,4,128]{2,1,0:T(4,128)S(1)}, u32[]{:S(2)}, u32[]{:S(2)}) collective-permute-start(f32[2,4,128]{2,1,0:T(4,128)S(1)} %get-tuple-element.57), channel_id=1, source_target_pairs={{0,1},{1,0},{2,3},{3,2},{4,5},{5,4},{6,7},{7,6},{8,9},{9,8},{10,11... | collective-permute-start | bytes 12296 | tf_op jit(solution)/shard_map/ppermute | solution.py:537
  64.4 0.0 copy-start.2
  64.5 0.1 collective-permute-start.14
  64.6 0.1 collective-permute-start.12
  64.6 7.2 %collective-permute-start.13 = (f32[2,128,128]{2,1,0:T(8,128)S(1)}, f32[2,128,128]{2,1,0:T(8,128)S(1)}, u32[]{:S(2)}, u32[]{:S(2)}) collective-permute-start(f32[2,128,128]{2,1,0:T(8,128)S(1)} %get-tuple-element.55), channel_id=1, source_target_pairs={{4,0},{8,4},{12,8},{16,12},{20,16},{24,20},{28,24},{32,28},{36,32}... | collective-permute-start | bytes 393224 | tf_op jit(solution)/shard_map/ppermute | solution.py:535
  71.8 0.0 collective-permute-done.15
  71.8 0.0 copy-done.2
  71.8 0.0 collective-permute-done.14
  71.9 0.6 copy.17
  72.5 0.6 copy.16
  73.1 2.4 %collective-permute-done.12 = f32[2,128,128]{2,1,0:T(8,128)S(1)} collective-permute-done((f32[2,128,128]{2,1,0:T(8,128)S(1)}, f32[2,128,128]{2,1,0:T(8,128)S(1)}, u32[]{:S(2)}, u32[]{:S(2)}) %collective-permute-start.12) | collective-permute-done | bytes 131104 | tf_op jit(solution)/shard_map/ppermute | solution.py:534
  75.5 0.0 collective-permute-done.13
  75.5 0.0 copy-done.5
  75.5 0.7 pad_maximum_fusion
  (6 shorter events, 0.1 us)
Async XLA Ops:
  1.3 0.7 copy-start.3
  1.3 0.7 copy-start.4
  2.0 0.7 copy-start
  2.6 0.7 copy-start.1
  8.6 15.3 %collective-permute-start = (f32[256,128]{1,0:T(8,128)S(1)}, f32[256,128]{1,0:T(8,128)S(1)}, u32[]{:S(2)}, u32[]{:S(2)}) collective-permute-start(f32[256,128]{1,0:T(8,128)S(1)} %get-tuple-element.41), channel_id=1, source_target_pairs={{0,4},{4,8},{8,12},{12,16},{16,20},{20,24},{24,28},{28,32},{32,36}... | collective-permute-start | bytes 393224 | tf_op jit(solution)/shard_map/ppermute | solution.py:534
  13.1 10.8 %collective-permute-start.1 = (f32[256,128]{1,0:T(8,128)S(1)}, f32[256,128]{1,0:T(8,128)S(1)}, u32[]{:S(2)}, u32[]{:S(2)}) collective-permute-start(f32[256,128]{1,0:T(8,128)S(1)} %get-tuple-element.42), channel_id=1, source_target_pairs={{4,0},{8,4},{12,8},{16,12},{20,16},{24,20},{28,24},{32,28},{36,32}... | collective-permute-start | bytes 393224 | tf_op jit(solution)/shard_map/ppermute | solution.py:535
  19.9 2.9 %collective-permute-start.2 = (f32[16,128]{1,0:T(8,128)S(1)}, f32[16,128]{1,0:T(8,128)S(1)}, u32[]{:S(2)}, u32[]{:S(2)}) collective-permute-start(f32[16,128]{1,0:T(8,128)S(1)} %get-tuple-element.43), channel_id=1, source_target_pairs={{0,2},{2,0},{1,3},{3,1},{4,6},{6,4},{5,7},{7,5},{8,10},{10,8},{9,1... | collective-permute-start | bytes 24584 | tf_op jit(solution)/shard_map/ppermute | solution.py:536
  20.7 2.1 %collective-permute-start.3 = (f32[2,4,128]{2,1,0:T(4,128)S(1)}, f32[2,4,128]{2,1,0:T(4,128)S(1)}, u32[]{:S(2)}, u32[]{:S(2)}) collective-permute-start(f32[2,4,128]{2,1,0:T(4,128)S(1)} %get-tuple-element.44), channel_id=1, source_target_pairs={{0,1},{1,0},{2,3},{3,2},{4,5},{5,4},{6,7},{7,6},{8,9},{9,8},{10,11... | collective-permute-start | bytes 12296 | tf_op jit(solution)/shard_map/ppermute | solution.py:537
  26.8 12.3 %collective-permute-start.4 = (f32[256,128]{1,0:T(8,128)S(1)}, f32[256,128]{1,0:T(8,128)S(1)}, u32[]{:S(2)}, u32[]{:S(2)}) collective-permute-start(f32[256,128]{1,0:T(8,128)S(1)} %get-tuple-element.45), channel_id=1, source_target_pairs={{0,4},{4,8},{8,12},{12,16},{16,20},{20,24},{24,28},{28,32},{32,36}... | collective-permute-start | bytes 393224 | tf_op jit(solution)/shard_map/ppermute | solution.py:534
  26.9 12.2 %collective-permute-start.5 = (f32[256,128]{1,0:T(8,128)S(1)}, f32[256,128]{1,0:T(8,128)S(1)}, u32[]{:S(2)}, u32[]{:S(2)}) collective-permute-start(f32[256,128]{1,0:T(8,128)S(1)} %get-tuple-element.46), channel_id=1, source_target_pairs={{4,0},{8,4},{12,8},{16,12},{20,16},{24,20},{28,24},{32,28},{36,32}... | collective-permute-start | bytes 393224 | tf_op jit(solution)/shard_map/ppermute | solution.py:535
  36.1 3.0 %collective-permute-start.6 = (f32[16,128]{1,0:T(8,128)S(1)}, f32[16,128]{1,0:T(8,128)S(1)}, u32[]{:S(2)}, u32[]{:S(2)}) collective-permute-start(f32[16,128]{1,0:T(8,128)S(1)} %get-tuple-element.47), channel_id=1, source_target_pairs={{0,2},{2,0},{1,3},{3,1},{4,6},{6,4},{5,7},{7,5},{8,10},{10,8},{9,1... | collective-permute-start | bytes 24584 | tf_op jit(solution)/shard_map/ppermute | solution.py:536
  36.1 3.0 %collective-permute-start.7 = (f32[2,4,128]{2,1,0:T(4,128)S(1)}, f32[2,4,128]{2,1,0:T(4,128)S(1)}, u32[]{:S(2)}, u32[]{:S(2)}) collective-permute-start(f32[2,4,128]{2,1,0:T(4,128)S(1)} %get-tuple-element.48), channel_id=1, source_target_pairs={{0,1},{1,0},{2,3},{3,2},{4,5},{5,4},{6,7},{7,6},{8,9},{9,8},{10,11... | collective-permute-start | bytes 12296 | tf_op jit(solution)/shard_map/ppermute | solution.py:537
  42.0 13.5 %collective-permute-start.8 = (f32[256,128]{1,0:T(8,128)S(1)}, f32[256,128]{1,0:T(8,128)S(1)}, u32[]{:S(2)}, u32[]{:S(2)}) collective-permute-start(f32[256,128]{1,0:T(8,128)S(1)} %get-tuple-element.49), channel_id=1, source_target_pairs={{0,4},{4,8},{8,12},{12,16},{16,20},{20,24},{24,28},{28,32},{32,36}... | collective-permute-start | bytes 393224 | tf_op jit(solution)/shard_map/ppermute | solution.py:534
  42.0 13.5 %collective-permute-start.9 = (f32[256,128]{1,0:T(8,128)S(1)}, f32[256,128]{1,0:T(8,128)S(1)}, u32[]{:S(2)}, u32[]{:S(2)}) collective-permute-start(f32[256,128]{1,0:T(8,128)S(1)} %get-tuple-element.50), channel_id=1, source_target_pairs={{4,0},{8,4},{12,8},{16,12},{20,16},{24,20},{28,24},{32,28},{36,32}... | collective-permute-start | bytes 393224 | tf_op jit(solution)/shard_map/ppermute | solution.py:535
  50.7 4.8 %collective-permute-start.10 = (f32[16,128]{1,0:T(8,128)S(1)}, f32[16,128]{1,0:T(8,128)S(1)}, u32[]{:S(2)}, u32[]{:S(2)}) collective-permute-start(f32[16,128]{1,0:T(8,128)S(1)} %get-tuple-element.51), channel_id=1, source_target_pairs={{0,2},{2,0},{1,3},{3,1},{4,6},{6,4},{5,7},{7,5},{8,10},{10,8},{9,1... | collective-permute-start | bytes 24584 | tf_op jit(solution)/shard_map/ppermute | solution.py:536
  53.0 2.5 %collective-permute-start.11 = (f32[2,4,128]{2,1,0:T(4,128)S(1)}, f32[2,4,128]{2,1,0:T(4,128)S(1)}, u32[]{:S(2)}, u32[]{:S(2)}) collective-permute-start(f32[2,4,128]{2,1,0:T(4,128)S(1)} %get-tuple-element.52), channel_id=1, source_target_pairs={{0,1},{1,0},{2,3},{3,2},{4,5},{5,4},{6,7},{7,6},{8,9},{9,8},{10,11... | collective-permute-start | bytes 12296 | tf_op jit(solution)/shard_map/ppermute | solution.py:537
  55.5 20.0 %copy-start.5 = (f32[2,2,128,128]{3,2,1,0:T(8,128)S(1)}, f32[2,2,128,128]{3,2,1,0:T(8,128)}, u32[]{:S(2)}) copy-start(f32[2,2,128,128]{3,2,1,0:T(8,128)} %refs_5_.1) | copy-start | bytes 786436
  59.6 12.3 %collective-permute-start.15 = (f32[2,4,128]{2,1,0:T(4,128)S(1)}, f32[2,4,128]{2,1,0:T(4,128)S(1)}, u32[]{:S(2)}, u32[]{:S(2)}) collective-permute-start(f32[2,4,128]{2,1,0:T(4,128)S(1)} %get-tuple-element.57), channel_id=1, source_target_pairs={{0,1},{1,0},{2,3},{3,2},{4,5},{5,4},{6,7},{7,6},{8,9},{9,8},{10,11... | collective-permute-start | bytes 12296 | tf_op jit(solution)/shard_map/ppermute | solution.py:537
  64.4 7.4 %copy-start.2 = (f32[2,2,4,128]{3,2,1,0:T(4,128)S(1)}, f32[2,2,4,128]{3,2,1,0:T(4,128)}, u32[]{:S(2)}) copy-start(f32[2,2,4,128]{3,2,1,0:T(4,128)} %refs_7_.1) | copy-start | bytes 24580
  64.5 7.4 %collective-permute-start.14 = (f32[2,4,128]{2,1,0:T(4,128)S(1)}, f32[2,4,128]{2,1,0:T(4,128)S(1)}, u32[]{:S(2)}, u32[]{:S(2)}) collective-permute-start(f32[2,4,128]{2,1,0:T(4,128)S(1)} %get-tuple-element.56), channel_id=1, source_target_pairs={{0,2},{2,0},{1,3},{3,1},{4,6},{6,4},{5,7},{7,5},{8,10},{10,8},{9,1... | collective-permute-start | bytes 12296 | tf_op jit(solution)/shard_map/ppermute | solution.py:536
  64.6 10.9 %collective-permute-start.12 = (f32[2,128,128]{2,1,0:T(8,128)S(1)}, f32[2,128,128]{2,1,0:T(8,128)S(1)}, u32[]{:S(2)}, u32[]{:S(2)}) collective-permute-start(f32[2,128,128]{2,1,0:T(8,128)S(1)} %get-tuple-element.54), channel_id=1, source_target_pairs={{0,4},{4,8},{8,12},{12,16},{16,20},{20,24},{24,28},{28,32},{32,36}... | collective-permute-start | bytes 393224 | tf_op jit(solution)/shard_map/ppermute | solution.py:534
  64.6 10.8 %collective-permute-start.13 = (f32[2,128,128]{2,1,0:T(8,128)S(1)}, f32[2,128,128]{2,1,0:T(8,128)S(1)}, u32[]{:S(2)}, u32[]{:S(2)}) collective-permute-start(f32[2,128,128]{2,1,0:T(8,128)S(1)} %get-tuple-element.55), channel_id=1, source_target_pairs={{4,0},{8,4},{12,8},{16,12},{20,16},{24,20},{28,24},{32,28},{36,32}... | collective-permute-start | bytes 393224 | tf_op jit(solution)/shard_map/ppermute | solution.py:535

commit v2 on v1

--- a/solution.py
+++ b/solution.py
@@ -273,7 +273,9 @@
     lines, spare, turned_z, cols_z, sum_z = take(5)
 
     place_x, place_y, place_z = (lax.axis_index("gx"), lax.axis_index("gy"), lax.axis_index("gz"))
-    ends_x = (place_x == 0, place_x == lax.axis_size("gx") - 1)
+    planes_x = ((SPAN_X - 1) * place_z, (SPAN_X - 1) * (1 - place_z))
+    outer_x = [jnp.where(plane == 0, 0, lax.axis_size("gx") - 1) for plane in planes_x]
+    ends_x = [place_x == outer for outer in outer_x]
     lane, sub = lanes(), sublanes()
 
     if first:
@@ -294,7 +296,8 @@
             target[...] = source[...]
         for i in (5, 6, 7):
             copies[i].wait()
-        low_tiles, high_tiles = [split([(trace_x, (side, n)) for n in range(NT)], matrix) for side in range(2)]
+        sides = (place_z, 1 - place_z)
+        low_tiles, high_tiles = [split([(trace_x, (side, n)) for n in range(NT)], matrix) for side in sides]
         for n in range(NT):
             for j in range(TURN):
                 for z in range(2):
@@ -321,7 +324,7 @@
         steps = substeps[0]
     last_part = jnp.where(steps == 2, F32(p_robin), F32(2.0 * p_robin))
     mid_part = jnp.where(steps == 2, F32(p_robin), F32(0.0))
-    faces_x = ((0, face_low, out_low), (SPAN_X - 1, face_high, out_high))
+    faces_x = ((planes_x[0], face_low, out_high), (planes_x[1], face_high, out_low))
 
     turned_z[...] = jnp.zeros((SPAN, SPAN), F32)
     inner_z = 1 - place_z
@@ -374,7 +377,8 @@
                 tile = at_face(n, j, z)
                 for end, (x, data, _) in zip(ends_x, faces_x):
                     value = jnp.where(end, keep_x[tile, :], data[tile, :])
-                    load[at(j, x, z), :] = load[at(j, x, z), :] + value * scale[at(j, x, z), :]
+                    at_x_face = aligned(at(j, 0, z).start + 2 * SUB * x)
+                    load[at_x_face, :] = load[at_x_face, :] + value * scale[at_x_face, :]
 
         def substep(index, nothing):
             def to_res(j, here, total):
@@ -434,7 +438,7 @@
                 pair = []
                 for z in range(2):
                     tile = at_face(n, j, z)
-                    pair.append(mean(at(j, x, z).start, last_part, mid_part) - data[tile, :])
+                    pair.append(mean(at(j, 0, z).start + 2 * SUB * x, last_part, mid_part) - data[tile, :])
                     if not final:
                         out[tile, :] = pair[z]
                 made.append(pair)
@@ -521,18 +525,26 @@
         in_specs=in_specs,
         out_specs=[vmem] * len(shapes),
         scratch_shapes=scratch,
-        compiler_params=pltpu.CompilerParams(vmem_limit_bytes=(52 if first else 24) * 1024 * 1024),
+        compiler_params=pltpu.CompilerParams(vmem_limit_bytes=24 * 1024 * 1024),
     )(*operands)
 
 
 def exchange(out_low, out_high, out_y, out_z):
     count = lax.axis_size("gx")
-    up = [(i, (i + 1) % count) for i in range(count)]
-    down = [(j, i) for i, j in up]
+    cores = lax.axis_size("gz")
+
+    def turn(way):
+        pairs = []
+        for i in range(count):
+            for z in range(cores):
+                to = i + (way if z == 0 else -way)
+                pairs.append((i * cores + z, to * cores + z if 0 <= to < count else i * cores + 1 - z))
+        return pairs
+
     swap = [(0, 1), (1, 0)]
     return (
-        lax.ppermute(out_high, "gx", up),
-        lax.ppermute(out_low, "gx", down),
+        lax.ppermute(out_low, ("gx", "gz"), turn(1)),
+        lax.ppermute(out_high, ("gx", "gz"), turn(-1)),
         lax.ppermute(out_y, "gy", swap),
         lax.ppermute(out_z, "gz", swap),
     )
@@ -541,7 +553,10 @@
 def local(initial, material, conduct, capacity, substeps, trace_x, trace_y, trace_z):
     steps = substeps.reshape(1)
     place_x, place_y, place_z = (lax.axis_index("gx"), lax.axis_index("gy"), lax.axis_index("gz"))
-    results = solve(True, False, initial, material, conduct, capacity, steps, trace_x, trace_y, trace_z)
+    inputs = (initial, material, conduct, capacity, steps, trace_x, trace_y, trace_z)
+    hold = lambda value: pltpu.with_memory_space_constraint(value, pltpu.MemorySpace.HBM)
+    inputs = [value if value is steps else hold(value) for value in inputs]
+    results = solve(True, False, *inputs)
     prepared, sent = results[:10], results[10:]
     for iteration in range(1, ITERS):
         arrived = exchange(*sent)
@@ -549,6 +564,10 @@
         sent = solve(False, final, steps, *prepared, *arrived)
     field, *sent = sent
     face_low, face_high, come_y, come_z = exchange(*sent)
+    face_low, face_high = (
+        jnp.where(place_z == 0, face_low, face_high),
+        jnp.where(place_z == 0, face_high, face_low),
+    )
     face_low = jnp.where(place_x == 0, trace_x[0], face_low)
     face_high = jnp.where(place_x == lax.axis_size("gx") - 1, trace_x[1], face_high)
     got_x = jnp.stack([face_low, face_high], 0)

time: 76.4 us -> 74.7 us (0.978)
  the two profiles are of different devices: /device:TPU:1 before, /device:TPU:3 now
where the time goes in v2:
time: 74.7 us; the launch traced here: 75.2 us
  starting transfers between devices  41.8 us (56%)
  Pallas kernels  15.1 us (20%)
  waiting for transfers between devices  14.8 us (20%)
  between operations  1.4 us (2%)
  local copies, waits for them, and re-layouts  1.23 us (2%)
  other arithmetic  0.78 us (1%)
    ppermute x4, starting transfers between devices, exchange(): lax.ppermute(out_low, ('gx', 'gz'), turn(1))  19.4 us
    pallas_call x4, Pallas kernels, solve(): pl.pallas_call(functools.partial(kernel, first, final), out_shape=[jax.Sh...  15.1 us
    ppermute x4, starting transfers between devices, exchange(): lax.ppermute(out_z, 'gz', swap)  14.7 us
    ppermute x4, waiting for transfers between devices, exchange(): lax.ppermute(out_high, ('gx', 'gz'), turn(-1))  10.4 us
    ppermute x4, starting transfers between devices, exchange(): lax.ppermute(out_y, 'gy', swap)  5.82 us
    ppermute x4, waiting for transfers between devices, exchange(): lax.ppermute(out_z, 'gz', swap)  2.47 us
    ppermute x4, starting transfers between devices, exchange(): lax.ppermute(out_high, ('gx', 'gz'), turn(-1))  1.88 us
  transfers between devices with their start and end apart: 16, of which 8 were waited for; matrix products, arithmetic and copies ran while one was open for 2% of the time, Pallas kernels for 0%

profile of v2, /device:TPU:3, one launch (start us, length us, event | category | flops | bytes accessed | tf_op | source)
XLA Modules:
  0.0 75.2 jit_solution(13251773679233552599)
XLA Ops:
  1.3 5.3 %shard_map.111 = (f32[384,128]{1,0:T(8,128)S(1)}, f32[512,128]{1,0:T(8,128)S(1)}, f32[64,128]{1,0:T(8,128)S(1)}, f32[512,128]{1,0:T(8,128)S(1)}, f32[512,128]{1,...) custom-call(f32[4,128,128]{2,1,0:T(8,128)} %refs_0_.1, ...), custom_call_target="tpu_custom_call" | custom-call | tf_op jit(solution)/shard_map/pallas_call | solution.py:522
  6.6 8.2 %collective-permute-start = (f32[256,128]{1,0:T(8,128)S(1)}, f32[256,128]{1,0:T(8,128)S(1)}, u32[]{:S(2)}, u32[]{:S(2)}) collective-permute-start(f32[256,128]{1,0:T(8,128)S(1)} %get-tuple-element.41), channel_id=1, source_target_pairs={{0,4},{1,0},{4,8},{5,1},{8,12},{9,5},{12,16},{13,9},{16,20},{17,13... | collective-permute-start | bytes 393224 | tf_op jit(solution)/shard_map/ppermute | solution.py:546
  14.7 0.0 collective-permute-start.1
  14.7 0.0 collective-permute-start.2
  14.7 3.1 %collective-permute-start.3 = (f32[2,4,128]{2,1,0:T(4,128)S(1)}, f32[2,4,128]{2,1,0:T(4,128)S(1)}, u32[]{:S(2)}, u32[]{:S(2)}) collective-permute-start(f32[2,4,128]{2,1,0:T(4,128)S(1)} %get-tuple-element.44), channel_id=1, source_target_pairs={{0,1},{1,0},{2,3},{3,2},{4,5},{5,4},{6,7},{7,6},{8,9},{9,8},{10,11... | collective-permute-start | bytes 12296 | tf_op jit(solution)/shard_map/ppermute | solution.py:549
  17.8 0.8 %collective-permute-done.3.refs_14_ = f32[2,4,128]{2,1,0:T(4,128)S(1)} collective-permute-done((f32[2,4,128]{2,1,0:T(4,128)S(1)}, f32[2,4,128]{2,1,0:T(4,128)S(1)}, u32[]{:S(2)}, u32[]{:S(2)}) %collective-permute-start.3) | collective-permute-done | bytes 4128 | tf_op jit(solution)/shard_map/ppermute | solution.py:549
  18.7 0.8 %collective-permute-done.2.refs_13_ = f32[16,128]{1,0:T(8,128)S(1)} collective-permute-done((f32[16,128]{1,0:T(8,128)S(1)}, f32[16,128]{1,0:T(8,128)S(1)}, u32[]{:S(2)}, u32[]{:S(2)}) %collective-permute-start.2) | collective-permute-done | bytes 8224 | tf_op jit(solution)/shard_map/ppermute | solution.py:548
  19.5 0.0 collective-permute-done.refs_11_
  19.5 3.6 %collective-permute-done.1.refs_12_ = f32[256,128]{1,0:T(8,128)S(1)} collective-permute-done((f32[256,128]{1,0:T(8,128)S(1)}, f32[256,128]{1,0:T(8,128)S(1)}, u32[]{:S(2)}, u32[]{:S(2)}) %collective-permute-start.1) | collective-permute-done | bytes 131104 | tf_op jit(solution)/shard_map/ppermute | solution.py:547
  23.1 2.9 %shard_map.112 = (f32[256,128]{1,0:T(8,128)S(1)}, f32[256,128]{1,0:T(8,128)S(1)}, f32[16,128]{1,0:T(8,128)S(1)}, f32[2,4,128]{2,1,0:T(4,128)S(1)}) custom-call(s32[1]{0:T(128)} %bitcast.40.refs_0_, f32[384,128]{1,0:T(8,128)S(1)} %get-tuple-element.31.refs_1_, f32[512,128]{1,0:T(8,128)S(1)} %get-tuple-element.32.refs_2_, ...), custom_call_target="tpu_custom_call" | custom-call | tf_op jit(solution)/shard_map/pallas_call | solution.py:522
  25.9 2.6 %collective-permute-start.4 = (f32[256,128]{1,0:T(8,128)S(1)}, f32[256,128]{1,0:T(8,128)S(1)}, u32[]{:S(2)}, u32[]{:S(2)}) collective-permute-start(f32[256,128]{1,0:T(8,128)S(1)} %get-tuple-element.45), channel_id=1, source_target_pairs={{0,4},{1,0},{4,8},{5,1},{8,12},{9,5},{12,16},{13,9},{16,20},{17,13... | collective-permute-start | bytes 393224 | tf_op jit(solution)/shard_map/ppermute | solution.py:546
  28.5 0.5 collective-permute-start.5
  29.0 0.7 collective-permute-start.6
  29.7 5.4 %collective-permute-start.7 = (f32[2,4,128]{2,1,0:T(4,128)S(1)}, f32[2,4,128]{2,1,0:T(4,128)S(1)}, u32[]{:S(2)}, u32[]{:S(2)}) collective-permute-start(f32[2,4,128]{2,1,0:T(4,128)S(1)} %get-tuple-element.48), channel_id=1, source_target_pairs={{0,1},{1,0},{2,3},{3,2},{4,5},{5,4},{6,7},{7,6},{8,9},{9,8},{10,11... | collective-permute-start | bytes 12296 | tf_op jit(solution)/shard_map/ppermute | solution.py:549
  35.1 0.8 %collective-permute-done.7.refs_14_ = f32[2,4,128]{2,1,0:T(4,128)S(1)} collective-permute-done((f32[2,4,128]{2,1,0:T(4,128)S(1)}, f32[2,4,128]{2,1,0:T(4,128)S(1)}, u32[]{:S(2)}, u32[]{:S(2)}) %collective-permute-start.7) | collective-permute-done | bytes 4128 | tf_op jit(solution)/shard_map/ppermute | solution.py:549
  35.9 0.0 collective-permute-done.6.refs_13_
  35.9 0.0 collective-permute-done.4.refs_11_
  35.9 0.9 %collective-permute-done.5.refs_12_ = f32[256,128]{1,0:T(8,128)S(1)} collective-permute-done((f32[256,128]{1,0:T(8,128)S(1)}, f32[256,128]{1,0:T(8,128)S(1)}, u32[]{:S(2)}, u32[]{:S(2)}) %collective-permute-start.5) | collective-permute-done | bytes 131104 | tf_op jit(solution)/shard_map/ppermute | solution.py:547
  36.9 2.9 %shard_map.113 = (f32[256,128]{1,0:T(8,128)S(1)}, f32[256,128]{1,0:T(8,128)S(1)}, f32[16,128]{1,0:T(8,128)S(1)}, f32[2,4,128]{2,1,0:T(4,128)S(1)}) custom-call(s32[1]{0:T(128)} %bitcast.41.refs_0_, f32[384,128]{1,0:T(8,128)S(1)} %get-tuple-element.31.refs_1_, f32[512,128]{1,0:T(8,128)S(1)} %get-tuple-element.32.refs_2_, ...), custom_call_target="tpu_custom_call" | custom-call | tf_op jit(solution)/shard_map/pallas_call | solution.py:522
  39.7 2.6 %collective-permute-start.8 = (f32[256,128]{1,0:T(8,128)S(1)}, f32[256,128]{1,0:T(8,128)S(1)}, u32[]{:S(2)}, u32[]{:S(2)}) collective-permute-start(f32[256,128]{1,0:T(8,128)S(1)} %get-tuple-element.49), channel_id=1, source_target_pairs={{0,4},{1,0},{4,8},{5,1},{8,12},{9,5},{12,16},{13,9},{16,20},{17,13... | collective-permute-start | bytes 393224 | tf_op jit(solution)/shard_map/ppermute | solution.py:546
  42.3 1.4 %collective-permute-start.9 = (f32[256,128]{1,0:T(8,128)S(1)}, f32[256,128]{1,0:T(8,128)S(1)}, u32[]{:S(2)}, u32[]{:S(2)}) collective-permute-start(f32[256,128]{1,0:T(8,128)S(1)} %get-tuple-element.50), channel_id=1, source_target_pairs={{0,1},{1,5},{4,0},{5,9},{8,4},{9,13},{12,8},{13,17},{16,12},{17,21... | collective-permute-start | bytes 393224 | tf_op jit(solution)/shard_map/ppermute | solution.py:547
  43.7 1.5 %collective-permute-start.10 = (f32[16,128]{1,0:T(8,128)S(1)}, f32[16,128]{1,0:T(8,128)S(1)}, u32[]{:S(2)}, u32[]{:S(2)}) collective-permute-start(f32[16,128]{1,0:T(8,128)S(1)} %get-tuple-element.51), channel_id=1, source_target_pairs={{0,2},{2,0},{1,3},{3,1},{4,6},{6,4},{5,7},{7,5},{8,10},{10,8},{9,1... | collective-permute-start | bytes 24584 | tf_op jit(solution)/shard_map/ppermute | solution.py:548
  45.2 5.1 %collective-permute-start.11 = (f32[2,4,128]{2,1,0:T(4,128)S(1)}, f32[2,4,128]{2,1,0:T(4,128)S(1)}, u32[]{:S(2)}, u32[]{:S(2)}) collective-permute-start(f32[2,4,128]{2,1,0:T(4,128)S(1)} %get-tuple-element.52), channel_id=1, source_target_pairs={{0,1},{1,0},{2,3},{3,2},{4,5},{5,4},{6,7},{7,6},{8,9},{9,8},{10,11... | collective-permute-start | bytes 12296 | tf_op jit(solution)/shard_map/ppermute | solution.py:549
  50.3 0.8 %collective-permute-done.11.refs_14_ = f32[2,4,128]{2,1,0:T(4,128)S(1)} collective-permute-done((f32[2,4,128]{2,1,0:T(4,128)S(1)}, f32[2,4,128]{2,1,0:T(4,128)S(1)}, u32[]{:S(2)}, u32[]{:S(2)}) %collective-permute-start.11) | collective-permute-done | bytes 4128 | tf_op jit(solution)/shard_map/ppermute | solution.py:549
  51.1 0.0 collective-permute-done.10.refs_13_
  51.1 0.0 collective-permute-done.8.refs_11_
  51.1 0.0 collective-permute-done.9.refs_12_
  51.1 0.0 copy-start.1
  51.2 0.0 copy-start
  51.2 4.1 %shard_map.114 = (f32[4,128,128]{2,1,0:T(8,128)}, f32[2,128,128]{2,1,0:T(8,128)S(1)}, f32[2,128,128]{2,1,0:T(8,128)S(1)}, f32[2,4,128]{2,1,0:T(4,128)S(1)}, f32[2,4,128]{2,1,0:T(4,128)S(1)}) custom-call(s32[1]{0:T(128)} %bitcast.42.refs_0_, f32[384,128]{1,0:T(8,128)S(1)} %get-tuple-element.31.refs_1_, f32[512,128]{1,0:T(8,128)S(1)} %get-tuple-element.32.refs_2_, ...), custom_call_target="tpu_custom_call" | custom-call | tf_op jit(solution)/shard_map/pallas_call | solution.py:522
  55.2 1.1 %collective-permute-start.15 = (f32[2,4,128]{2,1,0:T(4,128)S(1)}, f32[2,4,128]{2,1,0:T(4,128)S(1)}, u32[]{:S(2)}, u32[]{:S(2)}) collective-permute-start(f32[2,4,128]{2,1,0:T(4,128)S(1)} %get-tuple-element.57), channel_id=1, source_target_pairs={{0,1},{1,0},{2,3},{3,2},{4,5},{5,4},{6,7},{7,6},{8,9},{9,8},{10,11... | collective-permute-start | bytes 12296 | tf_op jit(solution)/shard_map/ppermute | solution.py:549
  56.3 0.0 copy-done.1
  56.3 0.0 copy-start.2
  56.3 3.6 %collective-permute-start.14 = (f32[2,4,128]{2,1,0:T(4,128)S(1)}, f32[2,4,128]{2,1,0:T(4,128)S(1)}, u32[]{:S(2)}, u32[]{:S(2)}) collective-permute-start(f32[2,4,128]{2,1,0:T(4,128)S(1)} %get-tuple-element.56), channel_id=1, source_target_pairs={{0,2},{2,0},{1,3},{3,1},{4,6},{6,4},{5,7},{7,5},{8,10},{10,8},{9,1... | collective-permute-start | bytes 12296 | tf_op jit(solution)/shard_map/ppermute | solution.py:548
  59.9 6.1 %collective-permute-start.12 = (f32[2,128,128]{2,1,0:T(8,128)S(1)}, f32[2,128,128]{2,1,0:T(8,128)S(1)}, u32[]{:S(2)}, u32[]{:S(2)}) collective-permute-start(f32[2,128,128]{2,1,0:T(8,128)S(1)} %get-tuple-element.54), channel_id=1, source_target_pairs={{0,4},{1,0},{4,8},{5,1},{8,12},{9,5},{12,16},{13,9},{16,20},{17,13... | collective-permute-start | bytes 393224 | tf_op jit(solution)/shard_map/ppermute | solution.py:546
  66.1 0.0 collective-permute-start.13
  66.1 0.0 collective-permute-done.15
  66.1 0.0 copy-done.2
  66.1 0.0 collective-permute-done.14
  66.1 0.6 copy.17
  66.7 0.6 copy.16
  67.3 1.2 %collective-permute-done.12 = f32[2,128,128]{2,1,0:T(8,128)S(1)} collective-permute-done((f32[2,128,128]{2,1,0:T(8,128)S(1)}, f32[2,128,128]{2,1,0:T(8,128)S(1)}, u32[]{:S(2)}, u32[]{:S(2)}) %collective-permute-start.12) | collective-permute-done | bytes 131104 | tf_op jit(solution)/shard_map/ppermute | solution.py:546
  68.5 5.9 %collective-permute-done.13 = f32[2,128,128]{2,1,0:T(8,128)S(1)} collective-permute-done((f32[2,128,128]{2,1,0:T(8,128)S(1)}, f32[2,128,128]{2,1,0:T(8,128)S(1)}, u32[]{:S(2)}, u32[]{:S(2)}) %collective-permute-start.13) | collective-permute-done | bytes 131104 | tf_op jit(solution)/shard_map/ppermute | solution.py:547
  74.4 0.0 copy-done
  74.4 0.7 pad_maximum_fusion
  (6 shorter events, 0.1 us)
Async XLA Ops:
  6.6 13.0 %collective-permute-start = (f32[256,128]{1,0:T(8,128)S(1)}, f32[256,128]{1,0:T(8,128)S(1)}, u32[]{:S(2)}, u32[]{:S(2)}) collective-permute-start(f32[256,128]{1,0:T(8,128)S(1)} %get-tuple-element.41), channel_id=1, source_target_pairs={{0,4},{1,0},{4,8},{5,1},{8,12},{9,5},{12,16},{13,9},{16,20},{17,13... | collective-permute-start | bytes 393224 | tf_op jit(solution)/shard_map/ppermute | solution.py:546
  14.7 8.3 %collective-permute-start.1 = (f32[256,128]{1,0:T(8,128)S(1)}, f32[256,128]{1,0:T(8,128)S(1)}, u32[]{:S(2)}, u32[]{:S(2)}) collective-permute-start(f32[256,128]{1,0:T(8,128)S(1)} %get-tuple-element.42), channel_id=1, source_target_pairs={{0,1},{1,5},{4,0},{5,9},{8,4},{9,13},{12,8},{13,17},{16,12},{17,21... | collective-permute-start | bytes 393224 | tf_op jit(solution)/shard_map/ppermute | solution.py:547
  14.7 4.8 %collective-permute-start.2 = (f32[16,128]{1,0:T(8,128)S(1)}, f32[16,128]{1,0:T(8,128)S(1)}, u32[]{:S(2)}, u32[]{:S(2)}) collective-permute-start(f32[16,128]{1,0:T(8,128)S(1)} %get-tuple-element.43), channel_id=1, source_target_pairs={{0,2},{2,0},{1,3},{3,1},{4,6},{6,4},{5,7},{7,5},{8,10},{10,8},{9,1... | collective-permute-start | bytes 24584 | tf_op jit(solution)/shard_map/ppermute | solution.py:548
  14.7 3.9 %collective-permute-start.3 = (f32[2,4,128]{2,1,0:T(4,128)S(1)}, f32[2,4,128]{2,1,0:T(4,128)S(1)}, u32[]{:S(2)}, u32[]{:S(2)}) collective-permute-start(f32[2,4,128]{2,1,0:T(4,128)S(1)} %get-tuple-element.44), channel_id=1, source_target_pairs={{0,1},{1,0},{2,3},{3,2},{4,5},{5,4},{6,7},{7,6},{8,9},{9,8},{10,11... | collective-permute-start | bytes 12296 | tf_op jit(solution)/shard_map/ppermute | solution.py:549
  25.9 10.0 %collective-permute-start.4 = (f32[256,128]{1,0:T(8,128)S(1)}, f32[256,128]{1,0:T(8,128)S(1)}, u32[]{:S(2)}, u32[]{:S(2)}) collective-permute-start(f32[256,128]{1,0:T(8,128)S(1)} %get-tuple-element.45), channel_id=1, source_target_pairs={{0,4},{1,0},{4,8},{5,1},{8,12},{9,5},{12,16},{13,9},{16,20},{17,13... | collective-permute-start | bytes 393224 | tf_op jit(solution)/shard_map/ppermute | solution.py:546
  28.5 8.3 %collective-permute-start.5 = (f32[256,128]{1,0:T(8,128)S(1)}, f32[256,128]{1,0:T(8,128)S(1)}, u32[]{:S(2)}, u32[]{:S(2)}) collective-permute-start(f32[256,128]{1,0:T(8,128)S(1)} %get-tuple-element.46), channel_id=1, source_target_pairs={{0,1},{1,5},{4,0},{5,9},{8,4},{9,13},{12,8},{13,17},{16,12},{17,21... | collective-permute-start | bytes 393224 | tf_op jit(solution)/shard_map/ppermute | solution.py:547
  29.0 6.9 %collective-permute-start.6 = (f32[16,128]{1,0:T(8,128)S(1)}, f32[16,128]{1,0:T(8,128)S(1)}, u32[]{:S(2)}, u32[]{:S(2)}) collective-permute-start(f32[16,128]{1,0:T(8,128)S(1)} %get-tuple-element.47), channel_id=1, source_target_pairs={{0,2},{2,0},{1,3},{3,1},{4,6},{6,4},{5,7},{7,5},{8,10},{10,8},{9,1... | collective-permute-start | bytes 24584 | tf_op jit(solution)/shard_map/ppermute | solution.py:548
  29.7 6.2 %collective-permute-start.7 = (f32[2,4,128]{2,1,0:T(4,128)S(1)}, f32[2,4,128]{2,1,0:T(4,128)S(1)}, u32[]{:S(2)}, u32[]{:S(2)}) collective-permute-start(f32[2,4,128]{2,1,0:T(4,128)S(1)} %get-tuple-element.48), channel_id=1, source_target_pairs={{0,1},{1,0},{2,3},{3,2},{4,5},{5,4},{6,7},{7,6},{8,9},{9,8},{10,11... | collective-permute-start | bytes 12296 | tf_op jit(solution)/shard_map/ppermute | solution.py:549
  39.7 11.4 %collective-permute-start.8 = (f32[256,128]{1,0:T(8,128)S(1)}, f32[256,128]{1,0:T(8,128)S(1)}, u32[]{:S(2)}, u32[]{:S(2)}) collective-permute-start(f32[256,128]{1,0:T(8,128)S(1)} %get-tuple-element.49), channel_id=1, source_target_pairs={{0,4},{1,0},{4,8},{5,1},{8,12},{9,5},{12,16},{13,9},{16,20},{17,13... | collective-permute-start | bytes 393224 | tf_op jit(solution)/shard_map/ppermute | solution.py:546
  42.3 8.8 %collective-permute-start.9 = (f32[256,128]{1,0:T(8,128)S(1)}, f32[256,128]{1,0:T(8,128)S(1)}, u32[]{:S(2)}, u32[]{:S(2)}) collective-permute-start(f32[256,128]{1,0:T(8,128)S(1)} %get-tuple-element.50), channel_id=1, source_target_pairs={{0,1},{1,5},{4,0},{5,9},{8,4},{9,13},{12,8},{13,17},{16,12},{17,21... | collective-permute-start | bytes 393224 | tf_op jit(solution)/shard_map/ppermute | solution.py:547
  43.7 7.4 %collective-permute-start.10 = (f32[16,128]{1,0:T(8,128)S(1)}, f32[16,128]{1,0:T(8,128)S(1)}, u32[]{:S(2)}, u32[]{:S(2)}) collective-permute-start(f32[16,128]{1,0:T(8,128)S(1)} %get-tuple-element.51), channel_id=1, source_target_pairs={{0,2},{2,0},{1,3},{3,1},{4,6},{6,4},{5,7},{7,5},{8,10},{10,8},{9,1... | collective-permute-start | bytes 24584 | tf_op jit(solution)/shard_map/ppermute | solution.py:548
  45.2 5.9 %collective-permute-start.11 = (f32[2,4,128]{2,1,0:T(4,128)S(1)}, f32[2,4,128]{2,1,0:T(4,128)S(1)}, u32[]{:S(2)}, u32[]{:S(2)}) collective-permute-start(f32[2,4,128]{2,1,0:T(4,128)S(1)} %get-tuple-element.52), channel_id=1, source_target_pairs={{0,1},{1,0},{2,3},{3,2},{4,5},{5,4},{6,7},{7,6},{8,9},{9,8},{10,11... | collective-permute-start | bytes 12296 | tf_op jit(solution)/shard_map/ppermute | solution.py:549
  51.1 5.2 %copy-start.1 = (f32[2,4,2,128]{3,2,1,0:T(2,128)S(1)}, f32[2,4,2,128]{3,2,1,0:T(2,128)}, u32[]{:S(2)}) copy-start(f32[2,4,2,128]{3,2,1,0:T(2,128)} %refs_6_.1) | copy-start | bytes 24580
  51.2 23.2 %copy-start = (f32[2,2,128,128]{3,2,1,0:T(8,128)S(1)}, f32[2,2,128,128]{3,2,1,0:T(8,128)}, u32[]{:S(2)}) copy-start(f32[2,2,128,128]{3,2,1,0:T(8,128)} %refs_5_.1) | copy-start | bytes 786436
  55.2 10.8 %collective-permute-start.15 = (f32[2,4,128]{2,1,0:T(4,128)S(1)}, f32[2,4,128]{2,1,0:T(4,128)S(1)}, u32[]{:S(2)}, u32[]{:S(2)}) collective-permute-start(f32[2,4,128]{2,1,0:T(4,128)S(1)} %get-tuple-element.57), channel_id=1, source_target_pairs={{0,1},{1,0},{2,3},{3,2},{4,5},{5,4},{6,7},{7,6},{8,9},{9,8},{10,11... | collective-permute-start | bytes 12296 | tf_op jit(solution)/shard_map/ppermute | solution.py:549
  56.3 9.7 %copy-start.2 = (f32[2,2,4,128]{3,2,1,0:T(4,128)S(1)}, f32[2,2,4,128]{3,2,1,0:T(4,128)}, u32[]{:S(2)}) copy-start(f32[2,2,4,128]{3,2,1,0:T(4,128)} %refs_7_.1) | copy-start | bytes 24580
  56.3 9.7 %collective-permute-start.14 = (f32[2,4,128]{2,1,0:T(4,128)S(1)}, f32[2,4,128]{2,1,0:T(4,128)S(1)}, u32[]{:S(2)}, u32[]{:S(2)}) collective-permute-start(f32[2,4,128]{2,1,0:T(4,128)S(1)} %get-tuple-element.56), channel_id=1, source_target_pairs={{0,2},{2,0},{1,3},{3,1},{4,6},{6,4},{5,7},{7,5},{8,10},{10,8},{9,1... | collective-permute-start | bytes 12296 | tf_op jit(solution)/shard_map/ppermute | solution.py:548
  59.9 8.6 %collective-permute-start.12 = (f32[2,128,128]{2,1,0:T(8,128)S(1)}, f32[2,128,128]{2,1,0:T(8,128)S(1)}, u32[]{:S(2)}, u32[]{:S(2)}) collective-permute-start(f32[2,128,128]{2,1,0:T(8,128)S(1)} %get-tuple-element.54), channel_id=1, source_target_pairs={{0,4},{1,0},{4,8},{5,1},{8,12},{9,5},{12,16},{13,9},{16,20},{17,13... | collective-permute-start | bytes 393224 | tf_op jit(solution)/shard_map/ppermute | solution.py:546
  66.1 8.3 %collective-permute-start.13 = (f32[2,128,128]{2,1,0:T(8,128)S(1)}, f32[2,128,128]{2,1,0:T(8,128)S(1)}, u32[]{:S(2)}, u32[]{:S(2)}) collective-permute-start(f32[2,128,128]{2,1,0:T(8,128)S(1)} %get-tuple-element.55), channel_id=1, source_target_pairs={{0,1},{1,5},{4,0},{5,9},{8,4},{9,13},{12,8},{13,17},{16,12},{17,21... | collective-permute-start | bytes 393224 | tf_op jit(solution)/shard_map/ppermute | solution.py:547

commit v3 on v2

--- a/solution.py
+++ b/solution.py
@@ -252,7 +252,7 @@
     take = lambda n: [refs.pop(0) for _ in range(n)]
     if first:
         far = take(8)
-        cx, cy, cw, cz, weight, scale, start, keep_x, keep_y, keep_z = take(10)
+        outer_y, cx, cy, cw, cz, weight, scale, start, keep_x, keep_y, keep_z = take(11)
     else:
         (substeps,) = take(1)
         cx, cy, cw, cz, weight, scale, start, keep_x, keep_y, keep_z = take(10)
@@ -309,6 +309,7 @@
             for x in range(SPAN_X):
                 keep_z[n, pl.ds(x, 1), :] = trace_z[n, place_z, pl.ds(x, 1), :]
                 come_z[n, pl.ds(x, 1), :] = trace_z[n, 1 - place_z, pl.ds(x, 1), :]
+                outer_y[n, pl.ds(x, 1), :] = trace_y[n, x, pl.ds(place_y, 1), :]
                 for side in range(2):
                     spare[pl.ds(SUB * side + SPAN_X * n + x, 1), :] = trace_y[n, x, pl.ds(side, 1), :]
         both = spare[pl.ds(0, 2 * SUB), :]
@@ -482,11 +483,7 @@
         for n in range(NT):
             for x in range(SPAN_X):
                 out_y[n, pl.ds(x, 1), :] = spare[pl.ds(2 * SUB + SPAN_X * n + x, 1), :]
-        planes = []
-        for x in range(SPAN_X):
-            made = [[field[at(j, x, z), :] * scale[at(j, x, z), :] for z in range(2)] for j in range(TURN)]
-            planes.append((field_out, (x,), made))
-        join(planes, back)
+        field_out[...] = field[...] * scale[...]
 
 
 def solve(first, final, *operands):
@@ -501,10 +498,10 @@
         in_specs = [smem] + [vmem] * 14
     shapes = []
     if first:
-        shapes += [wide(ROWS_X), wide(ROWS), wide(len(TILES) * SUB)] + [wide(ROWS)] * 4
+        shapes += [lines_z, wide(ROWS_X), wide(ROWS), wide(len(TILES) * SUB)] + [wide(ROWS)] * 4
         shapes += [wide(NT * ROWS_A), wide(NT * SUB), lines_z]
     if final:
-        shapes += [(SPAN_X, SPAN, SPAN)]
+        shapes += [wide(ROWS)]
     shapes += [(NT, SPAN, SPAN) if final else wide(NT * ROWS_A)] * 2
     shapes += [lines_z if final else wide(NT * SUB), lines_z]
     scratch = []
@@ -529,6 +526,14 @@
     )(*operands)
 
 
+def unfold(field, out):
+    planes = []
+    for x in range(SPAN_X):
+        made = [[field[at(j, x, z), :] for z in range(2)] for j in range(TURN)]
+        planes.append((out, (x,), made))
+    join(planes, pairing(True))
+
+
 def exchange(out_low, out_high, out_y, out_z):
     count = lax.axis_size("gx")
     cores = lax.axis_size("gz")
@@ -557,7 +562,8 @@
     hold = lambda value: pltpu.with_memory_space_constraint(value, pltpu.MemorySpace.HBM)
     inputs = [value if value is steps else hold(value) for value in inputs]
     results = solve(True, False, *inputs)
-    prepared, sent = results[:10], results[10:]
+    outer_y, *prepared = results[:11]
+    outer_z, sent = prepared[-1], results[11:]
     for iteration in range(1, ITERS):
         arrived = exchange(*sent)
         final = iteration == ITERS - 1
@@ -571,9 +577,17 @@
     face_low = jnp.where(place_x == 0, trace_x[0], face_low)
     face_high = jnp.where(place_x == lax.axis_size("gx") - 1, trace_x[1], face_high)
     got_x = jnp.stack([face_low, face_high], 0)
-    got_y = jnp.stack([jnp.where(place_y == side, trace_y[:, :, side], come_y) for side in range(2)], 2)
-    got_z = jnp.stack([jnp.where(place_z == side, trace_z[:, side], come_z) for side in range(2)], 1)
-    return (field, got_x, got_y, got_z)
+    got_y = jnp.stack([jnp.where(place_y == side, outer_y, come_y) for side in range(2)], 2)
+    got_z = jnp.stack([jnp.where(place_z == side, outer_z, come_z) for side in range(2)], 1)
+    vmem = pl.BlockSpec(memory_space=pltpu.VMEM)
+    thermal = pl.pallas_call(
+        unfold,
+        out_shape=jax.ShapeDtypeStruct((SPAN_X, SPAN, SPAN), F32),
+        in_specs=[vmem],
+        out_specs=vmem,
+        cost_estimate=pl.CostEstimate(flops=10**8, bytes_accessed=10**6, transcendentals=0),
+    )(pltpu.with_memory_space_constraint(field, pltpu.MemorySpace.VMEM))
+    return (thermal, got_x, got_y, got_z)
 
 
 def solution(mesh):

time: 74.7 us -> 73.1 us (0.979); the launches traced: 75.2 us -> 72.8 us
  starting transfers between devices: 41.8 us -> 27.6 us
  Pallas kernels: 15.1 us -> 23.5 us
  waiting for transfers between devices: 14.8 us -> 18.4 us
    pallas_call x4, Pallas kernels: 15.1 us -> 22.5 us  [solve(): pl.pallas_call(functools.partial(kernel, first, final), out_shape=[jax.Sh...]
    ppermute x4, starting transfers between devices: 14.7 us -> 8.8 us  [exchange(): lax.ppermute(out_z, 'gz', swap)]
    ppermute x4, starting transfers between devices: 5.82 us -> 0.44 us  [exchange(): lax.ppermute(out_y, 'gy', swap)]
    ppermute x4, starting transfers between devices: 19.4 us -> 14.4 us  [exchange(): lax.ppermute(out_low, ('gx', 'gz'), turn(1))]
    ppermute x4, waiting for transfers between devices: 10.4 us -> 15.1 us  [exchange(): lax.ppermute(out_high, ('gx', 'gz'), turn(-1))]
    ppermute x4, starting transfers between devices: 1.88 us -> 3.93 us  [exchange(): lax.ppermute(out_high, ('gx', 'gz'), turn(-1))]
    pallas_call x0 -> x1, Pallas kernels: none -> 0.98 us  [local(): pl.pallas_call(unfold, out_shape=jax.ShapeDtypeStruct((SPAN_X, SPAN, SPAN...]
  transfers between devices with their start and end apart: 16 -> 16, of which waited for: 8 -> 10; matrix products, arithmetic and copies ran while one was open for 2% -> 2% of each run, Pallas kernels for 0% -> 1%
where the time goes in v3:
time: 73.1 us; the launch traced here: 72.8 us
  starting transfers between devices  27.6 us (38%)
  Pallas kernels  23.5 us (32%)
  waiting for transfers between devices  18.4 us (25%)
  between operations  1.35 us (2%)
  local copies, waits for them, and re-layouts  1.21 us (2%)
  other arithmetic  0.78 us (1%)
    pallas_call x4, Pallas kernels, solve(): pl.pallas_call(functools.partial(kernel, first, final), out_shape=[jax.Sh...  22.5 us
    ppermute x4, waiting for transfers between devices, exchange(): lax.ppermute(out_high, ('gx', 'gz'), turn(-1))  15.1 us
    ppermute x4, starting transfers between devices, exchange(): lax.ppermute(out_low, ('gx', 'gz'), turn(1))  14.4 us
    ppermute x4, starting transfers between devices, exchange(): lax.ppermute(out_z, 'gz', swap)  8.8 us
    ppermute x4, starting transfers between devices, exchange(): lax.ppermute(out_high, ('gx', 'gz'), turn(-1))  3.93 us
    ppermute x4, waiting for transfers between devices, exchange(): lax.ppermute(out_z, 'gz', swap)  2.47 us
  transfers between devices with their start and end apart: 16, of which 10 were waited for; matrix products, arithmetic and copies ran while one was open for 2% of the time, Pallas kernels for 1%

profile of v3, /device:TPU:3, one launch (start us, length us, event | category | flops | bytes accessed | tf_op | source)
XLA Modules:
  0.0 72.8 jit_solution(8024211249321277679)
XLA Ops:
  1.3 7.4 %shard_map.111 = (f32[2,4,128]{2,1,0:T(4,128)S(1)}, f32[384,128]{1,0:T(8,128)S(1)}, f32[512,128]{1,0:T(8,128)S(1)}, f32[64,128]{1,0:T(8,128)S(1)}, f32[512,128]{...) custom-call(f32[4,128,128]{2,1,0:T(8,128)} %refs_0_.1, ...), custom_call_target="tpu_custom_call" | custom-call | tf_op jit(solution)/shard_map/pallas_call | solution.py:519
  8.7 6.1 %collective-permute-start = (f32[256,128]{1,0:T(8,128)S(1)}, f32[256,128]{1,0:T(8,128)S(1)}, u32[]{:S(2)}, u32[]{:S(2)}) collective-permute-start(f32[256,128]{1,0:T(8,128)S(1)} %get-tuple-element.42), channel_id=1, source_target_pairs={{0,4},{1,0},{4,8},{5,1},{8,12},{9,5},{12,16},{13,9},{16,20},{17,13... | collective-permute-start | bytes 393224 | tf_op jit(solution)/shard_map/ppermute | solution.py:551
  14.7 0.0 collective-permute-start.1
  14.7 0.0 collective-permute-start.2
  14.7 3.1 %collective-permute-start.3 = (f32[2,4,128]{2,1,0:T(4,128)S(1)}, f32[2,4,128]{2,1,0:T(4,128)S(1)}, u32[]{:S(2)}, u32[]{:S(2)}) collective-permute-start(f32[2,4,128]{2,1,0:T(4,128)S(1)} %get-tuple-element.45), channel_id=1, source_target_pairs={{0,1},{1,0},{2,3},{3,2},{4,5},{5,4},{6,7},{7,6},{8,9},{9,8},{10,11... | collective-permute-start | bytes 12296 | tf_op jit(solution)/shard_map/ppermute | solution.py:554
  17.9 0.8 %collective-permute-done.3.refs_14_ = f32[2,4,128]{2,1,0:T(4,128)S(1)} collective-permute-done((f32[2,4,128]{2,1,0:T(4,128)S(1)}, f32[2,4,128]{2,1,0:T(4,128)S(1)}, u32[]{:S(2)}, u32[]{:S(2)}) %collective-permute-start.3) | collective-permute-done | bytes 4128 | tf_op jit(solution)/shard_map/ppermute | solution.py:554
  18.7 0.1 collective-permute-done.2.refs_13_
  18.8 0.0 collective-permute-done.refs_11_
  18.8 4.3 %collective-permute-done.1.refs_12_ = f32[256,128]{1,0:T(8,128)S(1)} collective-permute-done((f32[256,128]{1,0:T(8,128)S(1)}, f32[256,128]{1,0:T(8,128)S(1)}, u32[]{:S(2)}, u32[]{:S(2)}) %collective-permute-start.1) | collective-permute-done | bytes 131104 | tf_op jit(solution)/shard_map/ppermute | solution.py:552
  23.1 4.9 %shard_map.112 = (f32[256,128]{1,0:T(8,128)S(1)}, f32[256,128]{1,0:T(8,128)S(1)}, f32[16,128]{1,0:T(8,128)S(1)}, f32[2,4,128]{2,1,0:T(4,128)S(1)}) custom-call(s32[1]{0:T(128)} %bitcast.22.refs_0_, f32[384,128]{1,0:T(8,128)S(1)} %get-tuple-element.32.refs_1_, f32[512,128]{1,0:T(8,128)S(1)} %get-tuple-element.33.refs_2_, ...), custom_call_target="tpu_custom_call" | custom-call | tf_op jit(solution)/shard_map/pallas_call | solution.py:519
  28.0 0.9 %collective-permute-start.4 = (f32[256,128]{1,0:T(8,128)S(1)}, f32[256,128]{1,0:T(8,128)S(1)}, u32[]{:S(2)}, u32[]{:S(2)}) collective-permute-start(f32[256,128]{1,0:T(8,128)S(1)} %get-tuple-element.46), channel_id=1, source_target_pairs={{0,4},{1,0},{4,8},{5,1},{8,12},{9,5},{12,16},{13,9},{16,20},{17,13... | collective-permute-start | bytes 393224 | tf_op jit(solution)/shard_map/ppermute | solution.py:551
  28.9 2.2 %collective-permute-start.5 = (f32[256,128]{1,0:T(8,128)S(1)}, f32[256,128]{1,0:T(8,128)S(1)}, u32[]{:S(2)}, u32[]{:S(2)}) collective-permute-start(f32[256,128]{1,0:T(8,128)S(1)} %get-tuple-element.47), channel_id=1, source_target_pairs={{0,1},{1,5},{4,0},{5,9},{8,4},{9,13},{12,8},{13,17},{16,12},{17,21... | collective-permute-start | bytes 393224 | tf_op jit(solution)/shard_map/ppermute | solution.py:552
  31.1 0.0 collective-permute-start.6
  31.1 2.0 %collective-permute-start.7 = (f32[2,4,128]{2,1,0:T(4,128)S(1)}, f32[2,4,128]{2,1,0:T(4,128)S(1)}, u32[]{:S(2)}, u32[]{:S(2)}) collective-permute-start(f32[2,4,128]{2,1,0:T(4,128)S(1)} %get-tuple-element.49), channel_id=1, source_target_pairs={{0,1},{1,0},{2,3},{3,2},{4,5},{5,4},{6,7},{7,6},{8,9},{9,8},{10,11... | collective-permute-start | bytes 12296 | tf_op jit(solution)/shard_map/ppermute | solution.py:554
  33.1 0.8 %collective-permute-done.7.refs_14_ = f32[2,4,128]{2,1,0:T(4,128)S(1)} collective-permute-done((f32[2,4,128]{2,1,0:T(4,128)S(1)}, f32[2,4,128]{2,1,0:T(4,128)S(1)}, u32[]{:S(2)}, u32[]{:S(2)}) %collective-permute-start.7) | collective-permute-done | bytes 4128 | tf_op jit(solution)/shard_map/ppermute | solution.py:554
  33.9 0.0 collective-permute-done.6.refs_13_
  33.9 0.5 collective-permute-done.4.refs_11_
  34.4 2.8 %collective-permute-done.5.refs_12_ = f32[256,128]{1,0:T(8,128)S(1)} collective-permute-done((f32[256,128]{1,0:T(8,128)S(1)}, f32[256,128]{1,0:T(8,128)S(1)}, u32[]{:S(2)}, u32[]{:S(2)}) %collective-permute-start.5) | collective-permute-done | bytes 131104 | tf_op jit(solution)/shard_map/ppermute | solution.py:552
  37.2 4.9 %shard_map.113 = (f32[256,128]{1,0:T(8,128)S(1)}, f32[256,128]{1,0:T(8,128)S(1)}, f32[16,128]{1,0:T(8,128)S(1)}, f32[2,4,128]{2,1,0:T(4,128)S(1)}) custom-call(s32[1]{0:T(128)} %bitcast.23.refs_0_, f32[384,128]{1,0:T(8,128)S(1)} %get-tuple-element.32.refs_1_, f32[512,128]{1,0:T(8,128)S(1)} %get-tuple-element.33.refs_2_, ...), custom_call_target="tpu_custom_call" | custom-call | tf_op jit(solution)/shard_map/pallas_call | solution.py:519
  42.1 1.3 %collective-permute-start.8 = (f32[256,128]{1,0:T(8,128)S(1)}, f32[256,128]{1,0:T(8,128)S(1)}, u32[]{:S(2)}, u32[]{:S(2)}) collective-permute-start(f32[256,128]{1,0:T(8,128)S(1)} %get-tuple-element.50), channel_id=1, source_target_pairs={{0,4},{1,0},{4,8},{5,1},{8,12},{9,5},{12,16},{13,9},{16,20},{17,13... | collective-permute-start | bytes 393224 | tf_op jit(solution)/shard_map/ppermute | solution.py:551
  43.4 1.7 %collective-permute-start.9 = (f32[256,128]{1,0:T(8,128)S(1)}, f32[256,128]{1,0:T(8,128)S(1)}, u32[]{:S(2)}, u32[]{:S(2)}) collective-permute-start(f32[256,128]{1,0:T(8,128)S(1)} %get-tuple-element.51), channel_id=1, source_target_pairs={{0,1},{1,5},{4,0},{5,9},{8,4},{9,13},{12,8},{13,17},{16,12},{17,21... | collective-permute-start | bytes 393224 | tf_op jit(solution)/shard_map/ppermute | solution.py:552
  45.2 0.0 collective-permute-start.10
  45.2 3.6 %collective-permute-start.11 = (f32[2,4,128]{2,1,0:T(4,128)S(1)}, f32[2,4,128]{2,1,0:T(4,128)S(1)}, u32[]{:S(2)}, u32[]{:S(2)}) collective-permute-start(f32[2,4,128]{2,1,0:T(4,128)S(1)} %get-tuple-element.53), channel_id=1, source_target_pairs={{0,1},{1,0},{2,3},{3,2},{4,5},{5,4},{6,7},{7,6},{8,9},{9,8},{10,11... | collective-permute-start | bytes 12296 | tf_op jit(solution)/shard_map/ppermute | solution.py:554
  48.8 0.8 %collective-permute-done.11.refs_14_ = f32[2,4,128]{2,1,0:T(4,128)S(1)} collective-permute-done((f32[2,4,128]{2,1,0:T(4,128)S(1)}, f32[2,4,128]{2,1,0:T(4,128)S(1)}, u32[]{:S(2)}, u32[]{:S(2)}) %collective-permute-start.11) | collective-permute-done | bytes 4128 | tf_op jit(solution)/shard_map/ppermute | solution.py:554
  49.7 0.0 collective-permute-done.10.refs_13_
  49.7 0.0 collective-permute-done.8.refs_11_
  49.7 2.1 %collective-permute-done.9.refs_12_ = f32[256,128]{1,0:T(8,128)S(1)} collective-permute-done((f32[256,128]{1,0:T(8,128)S(1)}, f32[256,128]{1,0:T(8,128)S(1)}, u32[]{:S(2)}, u32[]{:S(2)}) %collective-permute-start.9) | collective-permute-done | bytes 131104 | tf_op jit(solution)/shard_map/ppermute | solution.py:552
  51.8 5.3 %shard_map.114 = (f32[512,128]{1,0:T(8,128)S(1)}, f32[2,128,128]{2,1,0:T(8,128)S(1)}, f32[2,128,128]{2,1,0:T(8,128)S(1)}, f32[2,4,128]{2,1,0:T(4,128)S(1)}, f32[2,4,128]{2,1,0:T(4,128)S(1)}) custom-call(s32[1]{0:T(128)} %bitcast.24.refs_0_, f32[384,128]{1,0:T(8,128)S(1)} %get-tuple-element.32.refs_1_, f32[512,128]{1,0:T(8,128)S(1)} %get-tuple-element.33.refs_2_, ...), custom_call_target="tpu_custom_call" | custom-call | tf_op jit(solution)/shard_map/pallas_call | solution.py:519
  57.0 0.1 collective-permute-start.15
  57.1 0.4 collective-permute-start.14
  57.5 6.1 %collective-permute-start.12 = (f32[2,128,128]{2,1,0:T(8,128)S(1)}, f32[2,128,128]{2,1,0:T(8,128)S(1)}, u32[]{:S(2)}, u32[]{:S(2)}) collective-permute-start(f32[2,128,128]{2,1,0:T(8,128)S(1)} %get-tuple-element.55), channel_id=1, source_target_pairs={{0,4},{1,0},{4,8},{5,1},{8,12},{9,5},{12,16},{13,9},{16,20},{17,13... | collective-permute-start | bytes 393224 | tf_op jit(solution)/shard_map/ppermute | solution.py:551
  63.7 0.0 collective-permute-start.13
  63.7 0.0 copy-start
  63.7 1.0 %shard_map.115 = f32[4,128,128]{2,1,0:T(8,128)} custom-call(f32[512,128]{1,0:T(8,128)S(1)} %get-tuple-element.54.field), custom_call_target="tpu_custom_call" | custom-call | flops 100000000 | bytes 1000000 | tf_op jit(solution)/shard_map/pallas_call | solution.py:583
  64.7 0.0 collective-permute-done.15
  64.7 0.0 collective-permute-done.14
  64.7 0.6 copy.13
  65.3 0.6 copy.12
  65.9 0.1 collective-permute-done.12
  66.1 5.9 %collective-permute-done.13 = f32[2,128,128]{2,1,0:T(8,128)S(1)} collective-permute-done((f32[2,128,128]{2,1,0:T(8,128)S(1)}, f32[2,128,128]{2,1,0:T(8,128)S(1)}, u32[]{:S(2)}, u32[]{:S(2)}) %collective-permute-start.13) | collective-permute-done | bytes 131104 | tf_op jit(solution)/shard_map/ppermute | solution.py:552
  72.0 0.0 copy-done
  72.0 0.7 pad_maximum_fusion
  (5 shorter events, 0.1 us)
Async XLA Ops:
  8.7 10.2 %collective-permute-start = (f32[256,128]{1,0:T(8,128)S(1)}, f32[256,128]{1,0:T(8,128)S(1)}, u32[]{:S(2)}, u32[]{:S(2)}) collective-permute-start(f32[256,128]{1,0:T(8,128)S(1)} %get-tuple-element.42), channel_id=1, source_target_pairs={{0,4},{1,0},{4,8},{5,1},{8,12},{9,5},{12,16},{13,9},{16,20},{17,13... | collective-permute-start | bytes 393224 | tf_op jit(solution)/shard_map/ppermute | solution.py:551
  14.7 8.3 %collective-permute-start.1 = (f32[256,128]{1,0:T(8,128)S(1)}, f32[256,128]{1,0:T(8,128)S(1)}, u32[]{:S(2)}, u32[]{:S(2)}) collective-permute-start(f32[256,128]{1,0:T(8,128)S(1)} %get-tuple-element.43), channel_id=1, source_target_pairs={{0,1},{1,5},{4,0},{5,9},{8,4},{9,13},{12,8},{13,17},{16,12},{17,21... | collective-permute-start | bytes 393224 | tf_op jit(solution)/shard_map/ppermute | solution.py:552
  14.7 4.1 %collective-permute-start.2 = (f32[16,128]{1,0:T(8,128)S(1)}, f32[16,128]{1,0:T(8,128)S(1)}, u32[]{:S(2)}, u32[]{:S(2)}) collective-permute-start(f32[16,128]{1,0:T(8,128)S(1)} %get-tuple-element.44), channel_id=1, source_target_pairs={{0,2},{2,0},{1,3},{3,1},{4,6},{6,4},{5,7},{7,5},{8,10},{10,8},{9,1... | collective-permute-start | bytes 24584 | tf_op jit(solution)/shard_map/ppermute | solution.py:553
  14.7 3.9 %collective-permute-start.3 = (f32[2,4,128]{2,1,0:T(4,128)S(1)}, f32[2,4,128]{2,1,0:T(4,128)S(1)}, u32[]{:S(2)}, u32[]{:S(2)}) collective-permute-start(f32[2,4,128]{2,1,0:T(4,128)S(1)} %get-tuple-element.45), channel_id=1, source_target_pairs={{0,1},{1,0},{2,3},{3,2},{4,5},{5,4},{6,7},{7,6},{8,9},{9,8},{10,11... | collective-permute-start | bytes 12296 | tf_op jit(solution)/shard_map/ppermute | solution.py:554
  28.0 6.4 %collective-permute-start.4 = (f32[256,128]{1,0:T(8,128)S(1)}, f32[256,128]{1,0:T(8,128)S(1)}, u32[]{:S(2)}, u32[]{:S(2)}) collective-permute-start(f32[256,128]{1,0:T(8,128)S(1)} %get-tuple-element.46), channel_id=1, source_target_pairs={{0,4},{1,0},{4,8},{5,1},{8,12},{9,5},{12,16},{13,9},{16,20},{17,13... | collective-permute-start | bytes 393224 | tf_op jit(solution)/shard_map/ppermute | solution.py:551
  28.9 8.3 %collective-permute-start.5 = (f32[256,128]{1,0:T(8,128)S(1)}, f32[256,128]{1,0:T(8,128)S(1)}, u32[]{:S(2)}, u32[]{:S(2)}) collective-permute-start(f32[256,128]{1,0:T(8,128)S(1)} %get-tuple-element.47), channel_id=1, source_target_pairs={{0,1},{1,5},{4,0},{5,9},{8,4},{9,13},{12,8},{13,17},{16,12},{17,21... | collective-permute-start | bytes 393224 | tf_op jit(solution)/shard_map/ppermute | solution.py:552
  31.1 2.8 %collective-permute-start.6 = (f32[16,128]{1,0:T(8,128)S(1)}, f32[16,128]{1,0:T(8,128)S(1)}, u32[]{:S(2)}, u32[]{:S(2)}) collective-permute-start(f32[16,128]{1,0:T(8,128)S(1)} %get-tuple-element.48), channel_id=1, source_target_pairs={{0,2},{2,0},{1,3},{3,1},{4,6},{6,4},{5,7},{7,5},{8,10},{10,8},{9,1... | collective-permute-start | bytes 24584 | tf_op jit(solution)/shard_map/ppermute | solution.py:553
  31.1 2.8 %collective-permute-start.7 = (f32[2,4,128]{2,1,0:T(4,128)S(1)}, f32[2,4,128]{2,1,0:T(4,128)S(1)}, u32[]{:S(2)}, u32[]{:S(2)}) collective-permute-start(f32[2,4,128]{2,1,0:T(4,128)S(1)} %get-tuple-element.49), channel_id=1, source_target_pairs={{0,1},{1,0},{2,3},{3,2},{4,5},{5,4},{6,7},{7,6},{8,9},{9,8},{10,11... | collective-permute-start | bytes 12296 | tf_op jit(solution)/shard_map/ppermute | solution.py:554
  42.1 7.5 %collective-permute-start.8 = (f32[256,128]{1,0:T(8,128)S(1)}, f32[256,128]{1,0:T(8,128)S(1)}, u32[]{:S(2)}, u32[]{:S(2)}) collective-permute-start(f32[256,128]{1,0:T(8,128)S(1)} %get-tuple-element.50), channel_id=1, source_target_pairs={{0,4},{1,0},{4,8},{5,1},{8,12},{9,5},{12,16},{13,9},{16,20},{17,13... | collective-permute-start | bytes 393224 | tf_op jit(solution)/shard_map/ppermute | solution.py:551
  43.4 8.3 %collective-permute-start.9 = (f32[256,128]{1,0:T(8,128)S(1)}, f32[256,128]{1,0:T(8,128)S(1)}, u32[]{:S(2)}, u32[]{:S(2)}) collective-permute-start(f32[256,128]{1,0:T(8,128)S(1)} %get-tuple-element.51), channel_id=1, source_target_pairs={{0,1},{1,5},{4,0},{5,9},{8,4},{9,13},{12,8},{13,17},{16,12},{17,21... | collective-permute-start | bytes 393224 | tf_op jit(solution)/shard_map/ppermute | solution.py:552
  45.2 4.5 %collective-permute-start.10 = (f32[16,128]{1,0:T(8,128)S(1)}, f32[16,128]{1,0:T(8,128)S(1)}, u32[]{:S(2)}, u32[]{:S(2)}) collective-permute-start(f32[16,128]{1,0:T(8,128)S(1)} %get-tuple-element.52), channel_id=1, source_target_pairs={{0,2},{2,0},{1,3},{3,1},{4,6},{6,4},{5,7},{7,5},{8,10},{10,8},{9,1... | collective-permute-start | bytes 24584 | tf_op jit(solution)/shard_map/ppermute | solution.py:553
  45.2 4.5 %collective-permute-start.11 = (f32[2,4,128]{2,1,0:T(4,128)S(1)}, f32[2,4,128]{2,1,0:T(4,128)S(1)}, u32[]{:S(2)}, u32[]{:S(2)}) collective-permute-start(f32[2,4,128]{2,1,0:T(4,128)S(1)} %get-tuple-element.53), channel_id=1, source_target_pairs={{0,1},{1,0},{2,3},{3,2},{4,5},{5,4},{6,7},{7,6},{8,9},{9,8},{10,11... | collective-permute-start | bytes 12296 | tf_op jit(solution)/shard_map/ppermute | solution.py:554
  57.0 7.6 %collective-permute-start.15 = (f32[2,4,128]{2,1,0:T(4,128)S(1)}, f32[2,4,128]{2,1,0:T(4,128)S(1)}, u32[]{:S(2)}, u32[]{:S(2)}) collective-permute-start(f32[2,4,128]{2,1,0:T(4,128)S(1)} %get-tuple-element.59), channel_id=1, source_target_pairs={{0,1},{1,0},{2,3},{3,2},{4,5},{5,4},{6,7},{7,6},{8,9},{9,8},{10,11... | collective-permute-start | bytes 12296 | tf_op jit(solution)/shard_map/ppermute | solution.py:554
  57.1 7.6 %collective-permute-start.14 = (f32[2,4,128]{2,1,0:T(4,128)S(1)}, f32[2,4,128]{2,1,0:T(4,128)S(1)}, u32[]{:S(2)}, u32[]{:S(2)}) collective-permute-start(f32[2,4,128]{2,1,0:T(4,128)S(1)} %get-tuple-element.58), channel_id=1, source_target_pairs={{0,2},{2,0},{1,3},{3,1},{4,6},{6,4},{5,7},{7,5},{8,10},{10,8},{9,1... | collective-permute-start | bytes 12296 | tf_op jit(solution)/shard_map/ppermute | solution.py:553
  57.5 8.5 %collective-permute-start.12 = (f32[2,128,128]{2,1,0:T(8,128)S(1)}, f32[2,128,128]{2,1,0:T(8,128)S(1)}, u32[]{:S(2)}, u32[]{:S(2)}) collective-permute-start(f32[2,128,128]{2,1,0:T(8,128)S(1)} %get-tuple-element.55), channel_id=1, source_target_pairs={{0,4},{1,0},{4,8},{5,1},{8,12},{9,5},{12,16},{13,9},{16,20},{17,13... | collective-permute-start | bytes 393224 | tf_op jit(solution)/shard_map/ppermute | solution.py:551
  63.7 8.3 %collective-permute-start.13 = (f32[2,128,128]{2,1,0:T(8,128)S(1)}, f32[2,128,128]{2,1,0:T(8,128)S(1)}, u32[]{:S(2)}, u32[]{:S(2)}) collective-permute-start(f32[2,128,128]{2,1,0:T(8,128)S(1)} %get-tuple-element.56), channel_id=1, source_target_pairs={{0,1},{1,5},{4,0},{5,9},{8,4},{9,13},{12,8},{13,17},{16,12},{17,21... | collective-permute-start | bytes 393224 | tf_op jit(solution)/shard_map/ppermute | solution.py:552
  63.7 8.3 %copy-start = (f32[2,2,128,128]{3,2,1,0:T(8,128)S(1)}, f32[2,2,128,128]{3,2,1,0:T(8,128)}, u32[]{:S(2)}) copy-start(f32[2,2,128,128]{3,2,1,0:T(8,128)} %refs_5_.1) | copy-start | bytes 786436

commit v4 on v3

--- a/solution.py
+++ b/solution.py
@@ -463,7 +463,8 @@
             out_y[tile_y, :] = other_half(value)
         return nothing
 
-    lax.fori_loop(0, NT, coarse, 0)
+    for n in range(NT):
+        coarse(n, 0)
 
     for j in range(TURN):
         value = sum_z[pl.ds(SUB * j, SUB), :]

time: 73.1 us -> 72.3 us (0.989); the launches traced: 72.8 us -> 72.9 us
  Pallas kernels: 23.5 us -> 15.3 us
  starting transfers between devices: 27.6 us -> 33.6 us
  waiting for transfers between devices: 18.4 us -> 20.7 us
    ppermute x4, waiting for transfers between devices: 0.14 us -> 8.87 us  [exchange(): lax.ppermute(out_y, 'gy', swap)]
    pallas_call x4, Pallas kernels: 22.5 us -> 14.3 us  [solve(): pl.pallas_call(functools.partial(kernel, first, final), out_shape=[jax.Sh...]
    ppermute x4, starting transfers between devices: 0.44 us -> 7.15 us  [exchange(): lax.ppermute(out_y, 'gy', swap)]
    ppermute x4, waiting for transfers between devices: 15.1 us -> 9.03 us  [exchange(): lax.ppermute(out_high, ('gx', 'gz'), turn(-1))]
    ppermute x4, starting transfers between devices: 14.4 us -> 20 us  [exchange(): lax.ppermute(out_low, ('gx', 'gz'), turn(1))]
    ppermute x4, starting transfers between devices: 8.8 us -> 5.11 us  [exchange(): lax.ppermute(out_z, 'gz', swap)]
    ppermute x4, starting transfers between devices: 3.93 us -> 1.3 us  [exchange(): lax.ppermute(out_high, ('gx', 'gz'), turn(-1))]
  transfers between devices with their start and end apart: 16 -> 16, of which waited for: 10 -> 9; matrix products, arithmetic and copies ran while one was open for 2% -> 2% of each run, Pallas kernels for 1% -> 1%
where the time goes in v4:
time: 72.3 us; the launch traced here: 72.9 us
  starting transfers between devices  33.6 us (46%)
  waiting for transfers between devices  20.7 us (29%)
  Pallas kernels  15.3 us (21%)
  between operations  1.34 us (2%)
  local copies, waits for them, and re-layouts  1.21 us (2%)
  other arithmetic  0.78 us (1%)
    ppermute x4, starting transfers between devices, exchange(): lax.ppermute(out_low, ('gx', 'gz'), turn(1))  20 us
    pallas_call x4, Pallas kernels, solve(): pl.pallas_call(functools.partial(kernel, first, final), out_shape=[jax.Sh...  14.3 us
    ppermute x4, waiting for transfers between devices, exchange(): lax.ppermute(out_high, ('gx', 'gz'), turn(-1))  9.03 us
    ppermute x4, waiting for transfers between devices, exchange(): lax.ppermute(out_y, 'gy', swap)  8.87 us
    ppermute x4, starting transfers between devices, exchange(): lax.ppermute(out_y, 'gy', swap)  7.15 us
    ppermute x4, starting transfers between devices, exchange(): lax.ppermute(out_z, 'gz', swap)  5.11 us
    ppermute x4, waiting for transfers between devices, exchange(): lax.ppermute(out_z, 'gz', swap)  2.81 us
  transfers between devices with their start and end apart: 16, of which 9 were waited for; matrix products, arithmetic and copies ran while one was open for 2% of the time, Pallas kernels for 1%

profile of v4, /device:TPU:3, one launch (start us, length us, event | category | flops | bytes accessed | tf_op | source)
XLA Modules:
  0.0 72.9 jit_solution(8088600794333928923)
XLA Ops:
  1.3 5.3 %shard_map.111 = (f32[2,4,128]{2,1,0:T(4,128)S(1)}, f32[384,128]{1,0:T(8,128)S(1)}, f32[512,128]{1,0:T(8,128)S(1)}, f32[64,128]{1,0:T(8,128)S(1)}, f32[512,128]{...) custom-call(f32[4,128,128]{2,1,0:T(8,128)} %refs_0_.1, ...), custom_call_target="tpu_custom_call" | custom-call | tf_op jit(solution)/shard_map/pallas_call | solution.py:520
  6.6 8.4 %collective-permute-start = (f32[256,128]{1,0:T(8,128)S(1)}, f32[256,128]{1,0:T(8,128)S(1)}, u32[]{:S(2)}, u32[]{:S(2)}) collective-permute-start(f32[256,128]{1,0:T(8,128)S(1)} %get-tuple-element.42), channel_id=1, source_target_pairs={{0,4},{1,0},{4,8},{5,1},{8,12},{9,5},{12,16},{13,9},{16,20},{17,13... | collective-permute-start | bytes 393224 | tf_op jit(solution)/shard_map/ppermute | solution.py:552
  14.9 0.0 collective-permute-start.1
  14.9 0.7 %collective-permute-start.2 = (f32[16,128]{1,0:T(8,128)S(1)}, f32[16,128]{1,0:T(8,128)S(1)}, u32[]{:S(2)}, u32[]{:S(2)}) collective-permute-start(f32[16,128]{1,0:T(8,128)S(1)} %get-tuple-element.44), channel_id=1, source_target_pairs={{0,2},{2,0},{1,3},{3,1},{4,6},{6,4},{5,7},{7,5},{8,10},{10,8},{9,1... | collective-permute-start | bytes 24584 | tf_op jit(solution)/shard_map/ppermute | solution.py:554
  15.7 1.3 %collective-permute-start.3 = (f32[2,4,128]{2,1,0:T(4,128)S(1)}, f32[2,4,128]{2,1,0:T(4,128)S(1)}, u32[]{:S(2)}, u32[]{:S(2)}) collective-permute-start(f32[2,4,128]{2,1,0:T(4,128)S(1)} %get-tuple-element.45), channel_id=1, source_target_pairs={{0,1},{1,0},{2,3},{3,2},{4,5},{5,4},{6,7},{7,6},{8,9},{9,8},{10,11... | collective-permute-start | bytes 12296 | tf_op jit(solution)/shard_map/ppermute | solution.py:555
  17.0 0.8 %collective-permute-done.3.refs_14_ = f32[2,4,128]{2,1,0:T(4,128)S(1)} collective-permute-done((f32[2,4,128]{2,1,0:T(4,128)S(1)}, f32[2,4,128]{2,1,0:T(4,128)S(1)}, u32[]{:S(2)}, u32[]{:S(2)}) %collective-permute-start.3) | collective-permute-done | bytes 4128 | tf_op jit(solution)/shard_map/ppermute | solution.py:555
  17.8 3.2 %collective-permute-done.2.refs_13_ = f32[16,128]{1,0:T(8,128)S(1)} collective-permute-done((f32[16,128]{1,0:T(8,128)S(1)}, f32[16,128]{1,0:T(8,128)S(1)}, u32[]{:S(2)}, u32[]{:S(2)}) %collective-permute-start.2) | collective-permute-done | bytes 8224 | tf_op jit(solution)/shard_map/ppermute | solution.py:554
  21.0 0.0 collective-permute-done.refs_11_
  21.0 2.2 %collective-permute-done.1.refs_12_ = f32[256,128]{1,0:T(8,128)S(1)} collective-permute-done((f32[256,128]{1,0:T(8,128)S(1)}, f32[256,128]{1,0:T(8,128)S(1)}, u32[]{:S(2)}, u32[]{:S(2)}) %collective-permute-start.1) | collective-permute-done | bytes 131104 | tf_op jit(solution)/shard_map/ppermute | solution.py:553
  23.2 2.9 %shard_map.112 = (f32[256,128]{1,0:T(8,128)S(1)}, f32[256,128]{1,0:T(8,128)S(1)}, f32[16,128]{1,0:T(8,128)S(1)}, f32[2,4,128]{2,1,0:T(4,128)S(1)}) custom-call(s32[1]{0:T(128)} %bitcast.22.refs_0_, f32[384,128]{1,0:T(8,128)S(1)} %get-tuple-element.32.refs_1_, f32[512,128]{1,0:T(8,128)S(1)} %get-tuple-element.33.refs_2_, ...), custom_call_target="tpu_custom_call" | custom-call | tf_op jit(solution)/shard_map/pallas_call | solution.py:520
  26.2 2.9 %collective-permute-start.4 = (f32[256,128]{1,0:T(8,128)S(1)}, f32[256,128]{1,0:T(8,128)S(1)}, u32[]{:S(2)}, u32[]{:S(2)}) collective-permute-start(f32[256,128]{1,0:T(8,128)S(1)} %get-tuple-element.46), channel_id=1, source_target_pairs={{0,4},{1,0},{4,8},{5,1},{8,12},{9,5},{12,16},{13,9},{16,20},{17,13... | collective-permute-start | bytes 393224 | tf_op jit(solution)/shard_map/ppermute | solution.py:552
  29.0 0.2 collective-permute-start.5
  29.2 2.9 %collective-permute-start.6 = (f32[16,128]{1,0:T(8,128)S(1)}, f32[16,128]{1,0:T(8,128)S(1)}, u32[]{:S(2)}, u32[]{:S(2)}) collective-permute-start(f32[16,128]{1,0:T(8,128)S(1)} %get-tuple-element.48), channel_id=1, source_target_pairs={{0,2},{2,0},{1,3},{3,1},{4,6},{6,4},{5,7},{7,5},{8,10},{10,8},{9,1... | collective-permute-start | bytes 24584 | tf_op jit(solution)/shard_map/ppermute | solution.py:554
  32.2 0.0 collective-permute-start.7
  32.2 1.2 %collective-permute-done.7.refs_14_ = f32[2,4,128]{2,1,0:T(4,128)S(1)} collective-permute-done((f32[2,4,128]{2,1,0:T(4,128)S(1)}, f32[2,4,128]{2,1,0:T(4,128)S(1)}, u32[]{:S(2)}, u32[]{:S(2)}) %collective-permute-start.7) | collective-permute-done | bytes 4128 | tf_op jit(solution)/shard_map/ppermute | solution.py:555
  33.3 3.3 %collective-permute-done.6.refs_13_ = f32[16,128]{1,0:T(8,128)S(1)} collective-permute-done((f32[16,128]{1,0:T(8,128)S(1)}, f32[16,128]{1,0:T(8,128)S(1)}, u32[]{:S(2)}, u32[]{:S(2)}) %collective-permute-start.6) | collective-permute-done | bytes 8224 | tf_op jit(solution)/shard_map/ppermute | solution.py:554
  36.6 0.0 collective-permute-done.4.refs_11_
  36.6 0.7 %collective-permute-done.5.refs_12_ = f32[256,128]{1,0:T(8,128)S(1)} collective-permute-done((f32[256,128]{1,0:T(8,128)S(1)}, f32[256,128]{1,0:T(8,128)S(1)}, u32[]{:S(2)}, u32[]{:S(2)}) %collective-permute-start.5) | collective-permute-done | bytes 131104 | tf_op jit(solution)/shard_map/ppermute | solution.py:553
  37.4 3.1 %shard_map.113 = (f32[256,128]{1,0:T(8,128)S(1)}, f32[256,128]{1,0:T(8,128)S(1)}, f32[16,128]{1,0:T(8,128)S(1)}, f32[2,4,128]{2,1,0:T(4,128)S(1)}) custom-call(s32[1]{0:T(128)} %bitcast.23.refs_0_, f32[384,128]{1,0:T(8,128)S(1)} %get-tuple-element.32.refs_1_, f32[512,128]{1,0:T(8,128)S(1)} %get-tuple-element.33.refs_2_, ...), custom_call_target="tpu_custom_call" | custom-call | tf_op jit(solution)/shard_map/pallas_call | solution.py:520
  40.5 2.8 %collective-permute-start.8 = (f32[256,128]{1,0:T(8,128)S(1)}, f32[256,128]{1,0:T(8,128)S(1)}, u32[]{:S(2)}, u32[]{:S(2)}) collective-permute-start(f32[256,128]{1,0:T(8,128)S(1)} %get-tuple-element.50), channel_id=1, source_target_pairs={{0,4},{1,0},{4,8},{5,1},{8,12},{9,5},{12,16},{13,9},{16,20},{17,13... | collective-permute-start | bytes 393224 | tf_op jit(solution)/shard_map/ppermute | solution.py:552
  43.3 1.1 %collective-permute-start.9 = (f32[256,128]{1,0:T(8,128)S(1)}, f32[256,128]{1,0:T(8,128)S(1)}, u32[]{:S(2)}, u32[]{:S(2)}) collective-permute-start(f32[256,128]{1,0:T(8,128)S(1)} %get-tuple-element.51), channel_id=1, source_target_pairs={{0,1},{1,5},{4,0},{5,9},{8,4},{9,13},{12,8},{13,17},{16,12},{17,21... | collective-permute-start | bytes 393224 | tf_op jit(solution)/shard_map/ppermute | solution.py:553
  44.4 2.0 %collective-permute-start.10 = (f32[16,128]{1,0:T(8,128)S(1)}, f32[16,128]{1,0:T(8,128)S(1)}, u32[]{:S(2)}, u32[]{:S(2)}) collective-permute-start(f32[16,128]{1,0:T(8,128)S(1)} %get-tuple-element.52), channel_id=1, source_target_pairs={{0,2},{2,0},{1,3},{3,1},{4,6},{6,4},{5,7},{7,5},{8,10},{10,8},{9,1... | collective-permute-start | bytes 24584 | tf_op jit(solution)/shard_map/ppermute | solution.py:554
  46.4 2.5 %collective-permute-start.11 = (f32[2,4,128]{2,1,0:T(4,128)S(1)}, f32[2,4,128]{2,1,0:T(4,128)S(1)}, u32[]{:S(2)}, u32[]{:S(2)}) collective-permute-start(f32[2,4,128]{2,1,0:T(4,128)S(1)} %get-tuple-element.53), channel_id=1, source_target_pairs={{0,1},{1,0},{2,3},{3,2},{4,5},{5,4},{6,7},{7,6},{8,9},{9,8},{10,11... | collective-permute-start | bytes 12296 | tf_op jit(solution)/shard_map/ppermute | solution.py:555
  48.9 0.8 %collective-permute-done.11.refs_14_ = f32[2,4,128]{2,1,0:T(4,128)S(1)} collective-permute-done((f32[2,4,128]{2,1,0:T(4,128)S(1)}, f32[2,4,128]{2,1,0:T(4,128)S(1)}, u32[]{:S(2)}, u32[]{:S(2)}) %collective-permute-start.11) | collective-permute-done | bytes 4128 | tf_op jit(solution)/shard_map/ppermute | solution.py:555
  49.8 2.3 %collective-permute-done.10.refs_13_ = f32[16,128]{1,0:T(8,128)S(1)} collective-permute-done((f32[16,128]{1,0:T(8,128)S(1)}, f32[16,128]{1,0:T(8,128)S(1)}, u32[]{:S(2)}, u32[]{:S(2)}) %collective-permute-start.10) | collective-permute-done | bytes 8224 | tf_op jit(solution)/shard_map/ppermute | solution.py:554
  52.1 0.0 collective-permute-done.8.refs_11_
  52.1 0.0 collective-permute-done.9.refs_12_
  52.1 3.1 %shard_map.114 = (f32[512,128]{1,0:T(8,128)S(1)}, f32[2,128,128]{2,1,0:T(8,128)S(1)}, f32[2,128,128]{2,1,0:T(8,128)S(1)}, f32[2,4,128]{2,1,0:T(4,128)S(1)}, f32[2,4,128]{2,1,0:T(4,128)S(1)}) custom-call(s32[1]{0:T(128)} %bitcast.24.refs_0_, f32[384,128]{1,0:T(8,128)S(1)} %get-tuple-element.32.refs_1_, f32[512,128]{1,0:T(8,128)S(1)} %get-tuple-element.33.refs_2_, ...), custom_call_target="tpu_custom_call" | custom-call | tf_op jit(solution)/shard_map/pallas_call | solution.py:520
  55.1 1.3 %collective-permute-start.15 = (f32[2,4,128]{2,1,0:T(4,128)S(1)}, f32[2,4,128]{2,1,0:T(4,128)S(1)}, u32[]{:S(2)}, u32[]{:S(2)}) collective-permute-start(f32[2,4,128]{2,1,0:T(4,128)S(1)} %get-tuple-element.59), channel_id=1, source_target_pairs={{0,1},{1,0},{2,3},{3,2},{4,5},{5,4},{6,7},{7,6},{8,9},{9,8},{10,11... | collective-permute-start | bytes 12296 | tf_op jit(solution)/shard_map/ppermute | solution.py:555
  56.4 1.4 %collective-permute-start.14 = (f32[2,4,128]{2,1,0:T(4,128)S(1)}, f32[2,4,128]{2,1,0:T(4,128)S(1)}, u32[]{:S(2)}, u32[]{:S(2)}) collective-permute-start(f32[2,4,128]{2,1,0:T(4,128)S(1)} %get-tuple-element.58), channel_id=1, source_target_pairs={{0,2},{2,0},{1,3},{3,1},{4,6},{6,4},{5,7},{7,5},{8,10},{10,8},{9,1... | collective-permute-start | bytes 12296 | tf_op jit(solution)/shard_map/ppermute | solution.py:554
  57.9 6.0 %collective-permute-start.12 = (f32[2,128,128]{2,1,0:T(8,128)S(1)}, f32[2,128,128]{2,1,0:T(8,128)S(1)}, u32[]{:S(2)}, u32[]{:S(2)}) collective-permute-start(f32[2,128,128]{2,1,0:T(8,128)S(1)} %get-tuple-element.55), channel_id=1, source_target_pairs={{0,4},{1,0},{4,8},{5,1},{8,12},{9,5},{12,16},{13,9},{16,20},{17,13... | collective-permute-start | bytes 393224 | tf_op jit(solution)/shard_map/ppermute | solution.py:552
  63.8 0.0 collective-permute-start.13
  63.9 0.0 copy-start
  63.9 1.0 %shard_map.115 = f32[4,128,128]{2,1,0:T(8,128)} custom-call(f32[512,128]{1,0:T(8,128)S(1)} %get-tuple-element.54.field), custom_call_target="tpu_custom_call" | custom-call | flops 100000000 | bytes 1000000 | tf_op jit(solution)/shard_map/pallas_call | solution.py:584
  64.8 0.0 collective-permute-done.15
  64.8 0.0 collective-permute-done.14
  64.9 0.6 copy.13
  65.5 0.6 copy.12
  66.1 0.0 collective-permute-done.12
  66.1 6.1 %collective-permute-done.13 = f32[2,128,128]{2,1,0:T(8,128)S(1)} collective-permute-done((f32[2,128,128]{2,1,0:T(8,128)S(1)}, f32[2,128,128]{2,1,0:T(8,128)S(1)}, u32[]{:S(2)}, u32[]{:S(2)}) %collective-permute-start.13) | collective-permute-done | bytes 131104 | tf_op jit(solution)/shard_map/ppermute | solution.py:553
  72.2 0.0 copy-done
  72.2 0.7 pad_maximum_fusion
  (5 shorter events, 0.1 us)
Async XLA Ops:
  6.6 14.5 %collective-permute-start = (f32[256,128]{1,0:T(8,128)S(1)}, f32[256,128]{1,0:T(8,128)S(1)}, u32[]{:S(2)}, u32[]{:S(2)}) collective-permute-start(f32[256,128]{1,0:T(8,128)S(1)} %get-tuple-element.42), channel_id=1, source_target_pairs={{0,4},{1,0},{4,8},{5,1},{8,12},{9,5},{12,16},{13,9},{16,20},{17,13... | collective-permute-start | bytes 393224 | tf_op jit(solution)/shard_map/ppermute | solution.py:552
  14.9 8.3 %collective-permute-start.1 = (f32[256,128]{1,0:T(8,128)S(1)}, f32[256,128]{1,0:T(8,128)S(1)}, u32[]{:S(2)}, u32[]{:S(2)}) collective-permute-start(f32[256,128]{1,0:T(8,128)S(1)} %get-tuple-element.43), channel_id=1, source_target_pairs={{0,1},{1,5},{4,0},{5,9},{8,4},{9,13},{12,8},{13,17},{16,12},{17,21... | collective-permute-start | bytes 393224 | tf_op jit(solution)/shard_map/ppermute | solution.py:553
  14.9 6.1 %collective-permute-start.2 = (f32[16,128]{1,0:T(8,128)S(1)}, f32[16,128]{1,0:T(8,128)S(1)}, u32[]{:S(2)}, u32[]{:S(2)}) collective-permute-start(f32[16,128]{1,0:T(8,128)S(1)} %get-tuple-element.44), channel_id=1, source_target_pairs={{0,2},{2,0},{1,3},{3,1},{4,6},{6,4},{5,7},{7,5},{8,10},{10,8},{9,1... | collective-permute-start | bytes 24584 | tf_op jit(solution)/shard_map/ppermute | solution.py:554
  15.7 2.1 %collective-permute-start.3 = (f32[2,4,128]{2,1,0:T(4,128)S(1)}, f32[2,4,128]{2,1,0:T(4,128)S(1)}, u32[]{:S(2)}, u32[]{:S(2)}) collective-permute-start(f32[2,4,128]{2,1,0:T(4,128)S(1)} %get-tuple-element.45), channel_id=1, source_target_pairs={{0,1},{1,0},{2,3},{3,2},{4,5},{5,4},{6,7},{7,6},{8,9},{9,8},{10,11... | collective-permute-start | bytes 12296 | tf_op jit(solution)/shard_map/ppermute | solution.py:555
  26.2 10.5 %collective-permute-start.4 = (f32[256,128]{1,0:T(8,128)S(1)}, f32[256,128]{1,0:T(8,128)S(1)}, u32[]{:S(2)}, u32[]{:S(2)}) collective-permute-start(f32[256,128]{1,0:T(8,128)S(1)} %get-tuple-element.46), channel_id=1, source_target_pairs={{0,4},{1,0},{4,8},{5,1},{8,12},{9,5},{12,16},{13,9},{16,20},{17,13... | collective-permute-start | bytes 393224 | tf_op jit(solution)/shard_map/ppermute | solution.py:552
  29.0 8.3 %collective-permute-start.5 = (f32[256,128]{1,0:T(8,128)S(1)}, f32[256,128]{1,0:T(8,128)S(1)}, u32[]{:S(2)}, u32[]{:S(2)}) collective-permute-start(f32[256,128]{1,0:T(8,128)S(1)} %get-tuple-element.47), channel_id=1, source_target_pairs={{0,1},{1,5},{4,0},{5,9},{8,4},{9,13},{12,8},{13,17},{16,12},{17,21... | collective-permute-start | bytes 393224 | tf_op jit(solution)/shard_map/ppermute | solution.py:553
  29.2 7.4 %collective-permute-start.6 = (f32[16,128]{1,0:T(8,128)S(1)}, f32[16,128]{1,0:T(8,128)S(1)}, u32[]{:S(2)}, u32[]{:S(2)}) collective-permute-start(f32[16,128]{1,0:T(8,128)S(1)} %get-tuple-element.48), channel_id=1, source_target_pairs={{0,2},{2,0},{1,3},{3,1},{4,6},{6,4},{5,7},{7,5},{8,10},{10,8},{9,1... | collective-permute-start | bytes 24584 | tf_op jit(solution)/shard_map/ppermute | solution.py:554
  32.2 1.2 %collective-permute-start.7 = (f32[2,4,128]{2,1,0:T(4,128)S(1)}, f32[2,4,128]{2,1,0:T(4,128)S(1)}, u32[]{:S(2)}, u32[]{:S(2)}) collective-permute-start(f32[2,4,128]{2,1,0:T(4,128)S(1)} %get-tuple-element.49), channel_id=1, source_target_pairs={{0,1},{1,0},{2,3},{3,2},{4,5},{5,4},{6,7},{7,6},{8,9},{9,8},{10,11... | collective-permute-start | bytes 12296 | tf_op jit(solution)/shard_map/ppermute | solution.py:555
  40.5 11.6 %collective-permute-start.8 = (f32[256,128]{1,0:T(8,128)S(1)}, f32[256,128]{1,0:T(8,128)S(1)}, u32[]{:S(2)}, u32[]{:S(2)}) collective-permute-start(f32[256,128]{1,0:T(8,128)S(1)} %get-tuple-element.50), channel_id=1, source_target_pairs={{0,4},{1,0},{4,8},{5,1},{8,12},{9,5},{12,16},{13,9},{16,20},{17,13... | collective-permute-start | bytes 393224 | tf_op jit(solution)/shard_map/ppermute | solution.py:552
  43.3 8.8 %collective-permute-start.9 = (f32[256,128]{1,0:T(8,128)S(1)}, f32[256,128]{1,0:T(8,128)S(1)}, u32[]{:S(2)}, u32[]{:S(2)}) collective-permute-start(f32[256,128]{1,0:T(8,128)S(1)} %get-tuple-element.51), channel_id=1, source_target_pairs={{0,1},{1,5},{4,0},{5,9},{8,4},{9,13},{12,8},{13,17},{16,12},{17,21... | collective-permute-start | bytes 393224 | tf_op jit(solution)/shard_map/ppermute | solution.py:553
  44.4 7.7 %collective-permute-start.10 = (f32[16,128]{1,0:T(8,128)S(1)}, f32[16,128]{1,0:T(8,128)S(1)}, u32[]{:S(2)}, u32[]{:S(2)}) collective-permute-start(f32[16,128]{1,0:T(8,128)S(1)} %get-tuple-element.52), channel_id=1, source_target_pairs={{0,2},{2,0},{1,3},{3,1},{4,6},{6,4},{5,7},{7,5},{8,10},{10,8},{9,1... | collective-permute-start | bytes 24584 | tf_op jit(solution)/shard_map/ppermute | solution.py:554
  46.4 3.3 %collective-permute-start.11 = (f32[2,4,128]{2,1,0:T(4,128)S(1)}, f32[2,4,128]{2,1,0:T(4,128)S(1)}, u32[]{:S(2)}, u32[]{:S(2)}) collective-permute-start(f32[2,4,128]{2,1,0:T(4,128)S(1)} %get-tuple-element.53), channel_id=1, source_target_pairs={{0,1},{1,0},{2,3},{3,2},{4,5},{5,4},{6,7},{7,6},{8,9},{9,8},{10,11... | collective-permute-start | bytes 12296 | tf_op jit(solution)/shard_map/ppermute | solution.py:555
  55.1 9.7 %collective-permute-start.15 = (f32[2,4,128]{2,1,0:T(4,128)S(1)}, f32[2,4,128]{2,1,0:T(4,128)S(1)}, u32[]{:S(2)}, u32[]{:S(2)}) collective-permute-start(f32[2,4,128]{2,1,0:T(4,128)S(1)} %get-tuple-element.59), channel_id=1, source_target_pairs={{0,1},{1,0},{2,3},{3,2},{4,5},{5,4},{6,7},{7,6},{8,9},{9,8},{10,11... | collective-permute-start | bytes 12296 | tf_op jit(solution)/shard_map/ppermute | solution.py:555
  56.4 8.4 %collective-permute-start.14 = (f32[2,4,128]{2,1,0:T(4,128)S(1)}, f32[2,4,128]{2,1,0:T(4,128)S(1)}, u32[]{:S(2)}, u32[]{:S(2)}) collective-permute-start(f32[2,4,128]{2,1,0:T(4,128)S(1)} %get-tuple-element.58), channel_id=1, source_target_pairs={{0,2},{2,0},{1,3},{3,1},{4,6},{6,4},{5,7},{7,5},{8,10},{10,8},{9,1... | collective-permute-start | bytes 12296 | tf_op jit(solution)/shard_map/ppermute | solution.py:554
  57.9 8.2 %collective-permute-start.12 = (f32[2,128,128]{2,1,0:T(8,128)S(1)}, f32[2,128,128]{2,1,0:T(8,128)S(1)}, u32[]{:S(2)}, u32[]{:S(2)}) collective-permute-start(f32[2,128,128]{2,1,0:T(8,128)S(1)} %get-tuple-element.55), channel_id=1, source_target_pairs={{0,4},{1,0},{4,8},{5,1},{8,12},{9,5},{12,16},{13,9},{16,20},{17,13... | collective-permute-start | bytes 393224 | tf_op jit(solution)/shard_map/ppermute | solution.py:552
  63.8 8.3 %collective-permute-start.13 = (f32[2,128,128]{2,1,0:T(8,128)S(1)}, f32[2,128,128]{2,1,0:T(8,128)S(1)}, u32[]{:S(2)}, u32[]{:S(2)}) collective-permute-start(f32[2,128,128]{2,1,0:T(8,128)S(1)} %get-tuple-element.56), channel_id=1, source_target_pairs={{0,1},{1,5},{4,0},{5,9},{8,4},{9,13},{12,8},{13,17},{16,12},{17,21... | collective-permute-start | bytes 393224 | tf_op jit(solution)/shard_map/ppermute | solution.py:553
  63.9 8.3 %copy-start = (f32[2,2,128,128]{3,2,1,0:T(8,128)S(1)}, f32[2,2,128,128]{3,2,1,0:T(8,128)}, u32[]{:S(2)}) copy-start(f32[2,2,128,128]{3,2,1,0:T(8,128)} %refs_5_.1) | copy-start | bytes 786436
